TPU v7x, 512 devices: a whole 4x8x8 slice. The times are simulated.
512 devices in a mesh: expert: 8 (over y), dp: 64 (over z, x, core).
Axes of the slice: x: 4, y: 8, z: 8, core: 2. Of those that a mesh axis runs over, the one named last changes fastest.
Arguments:
- tokens: bfloat16 [16384, 2080], P('dp')
- grad_out: bfloat16 [16384, 3072], P('dp', 'expert')
- counts: int32 [64], P('dp'), may hold values from 8 to 256, as said below
- weight: bfloat16 [3072, 2080], P(('expert', 'dp')), may hold values from -3 to 3
- row_state: float32 [3072], P(('expert', 'dp')), may hold values from 0.01 to 0.75
- col_state: float32 [2080], replicated, may hold values from 0.05 to 0.5
Outputs:
- new_weight: bfloat16 [3072, 2080], P(('expert', 'dp'))
- new_rows: float32 [3072], P(('expert', 'dp'))
- new_cols: float32 [2080], replicated
Inputs may be any that keep to these rules, and one draw needn't show every extreme that they name: `counts`: each count is a multiple of 8; some index of dp has all 256 slots live in every draw.
All inputs are finite; a program needn't handle non-finite values.
Results may differ from a plain program's by a relative error of at most 0.001.
Values sent between devices are 32-bit elements; how exact they have to be, the bound alone decides.
A program may use at most 64 MiB of HBM per device.

v0:
```python
import jax
import jax.numpy as jnp
from jax import lax
from jax.sharding import PartitionSpec as P

D = 2080
FFW = 3072


def per_device(tokens, grad_out, counts, weight, row_state, col_state):
    rows_cap = tokens.shape[0]
    live = lax.broadcasted_iota(jnp.int32, (rows_cap, 1), 0) < counts[0]
    masked = jnp.where(live, grad_out, jnp.zeros_like(grad_out))
    contract = (((0,), (0,)), ((), ()))
    grad = lax.psum_scatter(
        lax.dot_general(masked, tokens, contract, preferred_element_type=jnp.float32),
        "dp",
        scatter_dimension=0,
        tiled=True,
    )
    squared = grad * grad
    row_mean = jnp.mean(squared, axis=1) + 1e-06
    new_rows = 0.5 * row_state + 0.5 * row_mean
    col_part = jnp.sum(squared, axis=0)
    row_part = jnp.sum(new_rows)
    col_total, row_total = lax.psum((col_part, row_part), ("expert", "dp"))
    new_cols = 0.5 * col_state + 0.5 * (col_total / FFW + 1e-06)
    row_avg = row_total / FFW
    update = grad / jnp.sqrt(new_rows[:, None] * new_cols[None, :] / row_avg)
    square_total = lax.psum(jnp.sum(update * update), ("expert", "dp"))
    rms_value = jnp.sqrt(square_total / (FFW * D))
    scaled = update / jnp.maximum(1.0, rms_value)
    new_weight = (weight.astype(jnp.float32) - 0.1 * scaled).astype(jnp.bfloat16)
    return (new_weight, new_rows, new_cols)


def solution(mesh):
    placed = (
        P("dp", None),
        P("dp", "expert"),
        P("dp"),
        P(("expert", "dp"), None),
        P(("expert", "dp")),
        P(),
    )
    return jax.shard_map(
        per_device,
        mesh=mesh,
        in_specs=placed,
        out_specs=(P(("expert", "dp"), None), P(("expert", "dp")), P()),
        check_vma=False,
    )
```

profile of v0, /device:TPU:1, one launch (start us, length us, event | category | flops | bytes accessed | tf_op | source)
XLA Modules:
  0.0 427.6 jit_solution(8247676942751747816)
XLA Ops:
  7.2 0.0 copy-start
  7.2 0.0 all-reduce.4.cloned.1.call-start
  8.0 0.5 copy-done
  8.4 0.0 copy-start.5
  8.4 0.0 copy-start.3
  8.4 0.0 copy-start.2
  8.4 3.4 fusion
  11.9 0.0 all-reduce.4.cloned.1.call-update
  11.9 1.3 dynamic-slice
  13.8 207.4 %all-reduce.4.cloned.1.call-done = f32[384,2080]{1,0:T(8,128)} async-done(((f32[384,2080]{1,0:T(8,128)}), f32[384,2080]{1,0:T(8,128)}) %all-reduce.4.cloned.1.call-update) | async-done | bytes 3194896
  221.2 1.1 multiply_reduce_fusion.1
  222.3 0.0 copy-done.5
  222.3 0.6 fusion.5
  222.9 0.0 copy-start.4
  222.9 99.1 %all-reduce.1 = (f32[]{:T(128)}, f32[2080]{0:T(1024)S(1)}) all-reduce(f32[]{:T(128)} %get-tuple-element.7, f32[2080]{0:T(1024)S(1)} %get-tuple-element.3), channel_id=1, replica_groups=mesh['expert'=8,'dp'=64] {'expert','dp'}, use_global_device_ids=true, to_apply=%region_5.6 | all-reduce | flops 2081 | bytes 16648 | tf_op jit(solution)/shard_map/psum | solution.py:26
  322.0 0.0 copy-done.3
  322.0 0.0 copy-start.1
  322.7 1.6 multiply_reduce_fusion
  324.3 94.1 %psum.23 = f32[]{:T(128)} all-reduce(f32[]{:T(128)} %multiply_reduce_fusion), channel_id=1, replica_groups=mesh['expert'=8,'dp'=64] {'expert','dp'}, use_global_device_ids=true, to_apply=%region_7.8 | all-reduce | flops 1 | bytes 8 | tf_op jit(solution)/shard_map/psum | solution.py:30
  419.1 0.0 copy-done.2
  419.1 1.6 subtract_convert_fusion
  420.8 0.0 copy-done.4
  420.8 0.0 copy-done.1
  (2 shorter events, 0.0 us)
Async XLA Ops:
  7.2 1.3 copy-start
  7.2 214.1 %all-reduce.4.cloned.1.call-start = ((), (), s32[]{:S(2)}) async-start(), calls=%async_computation | async-start | bytes 6684672
  8.4 213.9 %copy-start.5 = (f32[6]{0:T(128)S(1)}, f32[6]{0:T(128)}, u32[]{:S(2)}) copy-start(f32[6]{0:T(128)} %param.10) | copy-start | bytes 76
  8.4 313.6 %copy-start.3 = (f32[2080]{0:T(1024)S(1)}, f32[2080]{0:T(1024)}, u32[]{:S(2)}) copy-start(f32[2080]{0:T(1024)} %param.11) | copy-start | bytes 24964
  8.4 410.7 %copy-start.2 = (bf16[6,2080]{1,0:T(8,128)(2,1)S(1)}, bf16[6,2080]{1,0:T(8,128)(2,1)}, u32[]{:S(2)}) copy-start(bf16[6,2080]{1,0:T(8,128)(2,1)} %param.9) | copy-start | bytes 74884
  222.9 197.8 %copy-start.4 = (f32[6]{0:T(128)}, f32[6]{0:T(128)S(1)}, u32[]{:S(2)}) copy-start(f32[6]{0:T(128)S(1)} %get-tuple-element.8) | copy-start | bytes 76
  322.0 98.7 %copy-start.1 = (f32[2080]{0:T(1024)}, f32[2080]{0:T(1024)S(1)}, u32[]{:S(2)}) copy-start(f32[2080]{0:T(1024)S(1)} %add_multiply_fusion) | copy-start | bytes 24964
Sparse Core Ops, SparseCore 0:
  12.0 209.1 all-reduce.3
where the time goes:
time: 429 us; the launch traced here: 428 us
  waiting for transfers between devices  207 us (48%)
  blocking collectives  193 us (45%)
  between operations  16.8 us (4%)
  other arithmetic  4.91 us (1%)
    unnamed x2, waiting for transfers between devices  207 us
    psum x1, blocking collectives, per_device(): col_total, row_total = lax.psum((col_part, row_part), ('expert', 'dp'))  99.1 us
    psum x1, blocking collectives, per_device(): square_total = lax.psum(jnp.sum(update * update), ('expert', 'dp'))  94.1 us
  transfers between devices with their start and end apart: 1, of which 1 were waited for; matrix products, arithmetic and copies ran while one was open for 0% of the time, Pallas kernels for 0%

commit v1 on v0

v1 whole, which is shorter than its diff:
```python
import jax
import jax.numpy as jnp
import numpy as np
from jax import lax
from jax.experimental import pallas as pl
from jax.experimental.pallas import tpu as pltpu
from jax.sharding import PartitionSpec as P

D = 2080
FFW = 3072
NY, NZ, NX, NC = 8, 8, 4, 2
OWN = 6
ROWS = NC * OWN
WIDE = 1024
PART = 16
HALF = WIDE + 128
MESH = pl.DeviceIdType.MESH
F32 = jnp.float32


def row_order():
    pick = np.zeros((384, 384), np.float32)
    for x in range(NX):
        for z in range(NZ):
            for k in range(ROWS):
                pick[(x * NZ + z) * ROWS + k, (z * NX + x) * ROWS + k] = 1
    return pick


def kernel(
    tok_ref, go_ref, cnt_ref, w_ref, rs_ref, cs_ref, pick_ref,
    nw_ref, nr_ref, nc_ref,
    tok2, lhs, other, acc, core_in, d2_in, d1_in, z_in, g_own, g_sib, r_own, r_sib,
    st_y, st_z, st_x, st_sum, st_sib, wide, gwide,
    core_s, core_r, d2_s, d2_r, d1_s, d1_r, zs, zr, gs, gr, ys, yr, z2s, z2r, xs, xr,
):
    e = lax.axis_index("expert")
    q = lax.axis_index("dp")
    c, x, z = q % 2, (q // 2) % NX, q // (2 * NX)

    def at(ee, zz, xx, cc):
        return (ee, (zz * NX + xx) * 2 + cc)

    sib = at(e, z, x, 1 - c)
    y_peers = [at((e + d) % NY, z, x, c) for d in range(1, NY)]
    z_peers = [at(e, (z + d) % NZ, x, c) for d in range(1, NZ)]
    x_peers = [at(e, z, (x + d) % NX, c) for d in range(1, NX)]
    right, left = x_peers[0], x_peers[2]

    barrier = pltpu.get_barrier_semaphore()
    everyone = [sib] + y_peers + z_peers + x_peers
    for peer in everyone:
        pl.semaphore_signal(barrier, inc=1, device_id=peer, device_id_type=MESH)

    def remote(src, dst, s, r, peer):
        return pltpu.make_async_remote_copy(
            src_ref=src, dst_ref=dst, send_sem=s, recv_sem=r, device_id=peer, device_id_type=MESH
        )

    live = lax.broadcasted_iota(jnp.int32, (256, 384), 0) < cnt_ref[0]
    masked = jnp.where(live, go_ref[...].astype(F32), 0.0).astype(jnp.bfloat16)
    lhs[...] = lax.dot_general(
        pick_ref[...], masked, (((1,), (1,)), ((), ())), preferred_element_type=F32
    ).astype(jnp.bfloat16).reshape(NX, 96, 256)
    tail = tok_ref[:, 2 * WIDE : D]
    for h in range(2):
        tok2[h, :, 0:WIDE] = tok_ref[:, h * WIDE : (h + 1) * WIDE]
        put = lax.broadcasted_iota(jnp.int32, (32, 128), 0) == lax.broadcasted_iota(jnp.int32, (32, 128), 1) + h * PART
        put &= lax.broadcasted_iota(jnp.int32, (32, 128), 1) < PART
        put = jnp.where(put, 1.0, 0.0).astype(jnp.bfloat16)
        tok2[h, :, WIDE:HALF] = jnp.dot(tail, put, preferred_element_type=F32).astype(jnp.bfloat16)

    def product(k, _):
        block = lhs[k]
        other[k] = jnp.dot(block, tok2[1 - c], preferred_element_type=F32).reshape(4, 24, HALF)
        acc[k] = jnp.dot(block, tok2[c], preferred_element_type=F32).reshape(4, 24, HALF)
        return 0

    lax.fori_loop(0, NX, product, 0)
    pl.semaphore_wait(barrier, len(everyone))

    slabs = [(x + 2) % NX, (x + 1) % NX, (x + 3) % NX, x]
    core = [remote(other.at[k], core_in.at[k], core_s.at[j], core_r.at[j], sib) for j, k in enumerate(slabs)]
    for cp in core:
        cp.start()

    def settle(j):
        core[j].wait_recv()
        acc[slabs[j]] += core_in[slabs[j]]

    pz = z // 2
    far, up, down = (pz + 2) % 4, (pz + 1) % 4, (pz + 3) % 4
    settle(0)
    started = []
    d2 = {}
    for side, peer, chunks in ((0, right, (far, down)), (1, left, (up, pz))):
        for i, p in enumerate(chunks):
            cp = remote(acc.at[slabs[0], p], d2_in.at[side, i], d2_s.at[side, i], d2_r.at[side, i], peer)
            cp.start()
            d2[side, i] = cp
            started.append(cp)
    d1 = {}

    def forward(side, i, p, merge):
        k = slabs[1 + side]
        if merge is not None:
            d2[side, merge].wait_recv()
            acc[k, p] += d2_in[side, merge]
        cp = remote(acc.at[k, p], d1_in.at[side, i], d1_s.at[side, i], d1_r.at[side, i], (right, left)[side])
        cp.start()
        d1[side, i] = cp
        started.append(cp)

    settle(1)
    forward(0, 0, up, None)
    settle(2)
    forward(1, 0, far, None)
    settle(3)
    forward(0, 1, far, 0)
    forward(1, 1, up, 0)
    forward(0, 2, pz, None)
    forward(1, 2, down, None)
    forward(0, 3, down, 1)
    forward(1, 3, pz, 1)

    h0 = z % 2

    def collect(p, i, j):
        d1[0, i].wait_recv()
        d1[1, j].wait_recv()
        acc[x, p] += d1_in[0, i] + d1_in[1, j]

    def deliver(p, h):
        to = 2 * p + h
        first = pl.multiple_of(8 * h, 8)
        cp = remote(acc.at[x, p, pl.ds(first, 16)], z_in.at[z], zs.at[to], zr.at[z], at(e, to, x, c))
        cp.start()
        started.append(cp)

    collect(far, 1, 0)
    deliver(far, 0)
    deliver(far, 1)
    collect(up, 0, 1)
    deliver(up, 0)
    deliver(up, 1)
    collect(pz, 2, 3)
    deliver(pz, 1 - h0)
    collect(down, 3, 2)
    deliver(down, 0)
    deliver(down, 1)
    total = acc[x, pz, pl.ds(pl.multiple_of(8 * h0, 8), 16), :]
    for d in (4, 3, 5, 2, 6, 7, 1):
        k = (z + d) % NZ
        remote(z_in.at[k], z_in.at[k], zs.at[k], zr.at[k], sib).wait_recv()
        total += z_in[k]
    moved = jnp.concatenate([total[4:16], total[0:4]], axis=0)
    row16 = lax.broadcasted_iota(jnp.int32, (16, 1), 0)
    grad = jnp.where(row16 < ROWS, jnp.where(h0 == 1, moved, total), 0.0)
    g_own[...] = grad

    squared = grad * grad
    lane = lax.broadcasted_iota(jnp.int32, (16, 128), 1)
    row = lax.broadcasted_iota(jnp.int32, (16, 128), 0)
    state = jnp.zeros((16, 128), F32)
    for k in range(OWN):
        state = jnp.where(row == c * OWN + k, rs_ref[k], state)
    r_own[...] = jnp.where(lane < 64, jnp.sum(squared, axis=1, keepdims=True), state)
    r_copy = remote(r_own, r_sib, gs.at[0], gr.at[0], sib)
    r_copy.start()
    g_copy = remote(g_own, g_sib, gs.at[1], gr.at[1], sib)
    g_copy.start()
    started += [r_copy, g_copy]
    col_part = jnp.sum(squared, axis=0, keepdims=True)
    r_copy.wait_recv()
    both = r_own[...] + r_sib[...]
    new_rows = 0.5 * both[:, 64:65] + 0.5 * (both[:, 0:1] / D + 1e-06)
    s_part = jnp.sum(squared / new_rows, axis=0, keepdims=True)
    row_part = jnp.sum(jnp.where(row16 < ROWS, new_rows, 0.0), axis=0, keepdims=True)

    for k in range(9):
        st_y[e, k : k + 1, :] = col_part[:, 128 * k : 128 * (k + 1)]
        st_y[e, 9 + k : 10 + k, :] = s_part[:, 128 * k : 128 * (k + 1)]
    st_y[e, 18:24, :] = jnp.broadcast_to(row_part, (6, 128))

    def exchange(buf, me, n, s, r, peers):
        for d in range(1, n):
            cp = remote(buf.at[me], buf.at[me], s.at[d], r.at[me], peers[d - 1])
            cp.start()
            started.append(cp)
        for d in range(1, n):
            k = (me + d) % n
            remote(buf.at[k], buf.at[k], s.at[0], r.at[k], sib).wait_recv()
        out = buf[0]
        for k in range(1, n):
            out += buf[k]
        return out

    st_z[z] = exchange(st_y, e, NY, ys, yr, y_peers)
    st_x[x] = exchange(st_z, z, NZ, z2s, z2r, z_peers)
    mine = exchange(st_x, x, NX, xs, xr, x_peers)
    st_sum[...] = mine
    last = remote(st_sum, st_sib, gs.at[2], gr.at[2], sib)
    last.start()
    started.append(last)

    def halves(own, sibling):
        return jnp.where(c == 0, own, sibling), jnp.where(c == 0, sibling, own)

    g_copy.wait_recv()
    picked = []
    for ref in (g_own, g_sib):
        v = ref[...]
        picked.append(jnp.where(c == 0, v[0:8], jnp.concatenate([v[6:14]], axis=0)))
    first, second = halves(*picked)
    gwide[:, 0:WIDE] = first[:, 0:WIDE]
    gwide[:, WIDE : 2 * WIDE] = second[:, 0:WIDE]
    gwide[:, 2 * WIDE :] = first[:, WIDE:] + pltpu.roll(second[:, WIDE:], PART, 1)
    rows8 = jnp.where(c == 0, new_rows[0:8], new_rows[6:14])
    eye = lax.broadcasted_iota(jnp.int32, (8, 128), 0) == lax.broadcasted_iota(jnp.int32, (8, 128), 1)
    nr_ref[...] = jnp.sum(jnp.where(eye, rows8, 0.0), axis=0)[0:OWN]

    last.wait_recv()
    first, second = halves(mine, st_sib[...])
    for k in range(8):
        for j in range(2):
            wide[j : j + 1, 128 * k : 128 * (k + 1)] = first[9 * j + k : 9 * j + k + 1]
            wide[j : j + 1, WIDE + 128 * k : WIDE + 128 * (k + 1)] = second[9 * j + k : 9 * j + k + 1]
    for j in range(2):
        wide[j : j + 1, 2 * WIDE :] = first[9 * j + 8 : 9 * j + 9] + pltpu.roll(second[9 * j + 8 : 9 * j + 9], PART, 1)
    row_avg = mine[18:19, 0:1] / FFW
    new_cols = 0.5 * cs_ref[...].reshape(1, D) + 0.5 * (wide[0:1, 0:D] / FFW + 1e-06)
    nc_ref[...] = new_cols.reshape(D)
    total_sq = row_avg * jnp.sum(wide[1:2, 0:D] / new_cols, axis=1, keepdims=True)
    rms = jnp.sqrt(total_sq / (FFW * D))
    factor = 0.1 / jnp.maximum(1.0, rms) * jnp.sqrt(row_avg)
    scaled = gwide[0:OWN, 0:D] * (lax.rsqrt(rows8[0:OWN]) * factor) * lax.rsqrt(new_cols)
    nw_ref[...] = (w_ref[...].astype(F32) - scaled).astype(jnp.bfloat16)

    for cp in core + started:
        cp.wait_send()


def per_device(tokens, grad_out, counts, weight, row_state, col_state):
    vmem = pl.BlockSpec(memory_space=pltpu.VMEM)
    smem = pl.BlockSpec(memory_space=pltpu.SMEM)
    dma = pltpu.SemaphoreType.DMA
    return pl.pallas_call(
        kernel,
        out_shape=(
            jax.ShapeDtypeStruct((OWN, D), jnp.bfloat16),
            jax.ShapeDtypeStruct((OWN,), F32),
            jax.ShapeDtypeStruct((D,), F32),
        ),
        in_specs=[vmem, vmem, smem, vmem, smem, vmem, vmem],
        out_specs=(vmem, vmem, vmem),
        scratch_shapes=[
            pltpu.VMEM((2, 256, HALF), jnp.bfloat16),
            pltpu.VMEM((NX, 96, 256), jnp.bfloat16),
            pltpu.VMEM((NX, 4, 24, HALF), F32),
            pltpu.VMEM((NX, 4, 24, HALF), F32),
            pltpu.VMEM((NX, 4, 24, HALF), F32),
            pltpu.VMEM((2, 2, 24, HALF), F32),
            pltpu.VMEM((2, 4, 24, HALF), F32),
            pltpu.VMEM((NZ, 16, HALF), F32),
            pltpu.VMEM((16, HALF), F32),
            pltpu.VMEM((16, HALF), F32),
            pltpu.VMEM((16, 128), F32),
            pltpu.VMEM((16, 128), F32),
            pltpu.VMEM((NY, 24, 128), F32),
            pltpu.VMEM((NZ, 24, 128), F32),
            pltpu.VMEM((NX, 24, 128), F32),
            pltpu.VMEM((24, 128), F32),
            pltpu.VMEM((24, 128), F32),
            pltpu.VMEM((8, 2 * WIDE + 128), F32),
            pltpu.VMEM((8, 2 * WIDE + 128), F32),
            dma((4,)), dma((4,)), dma((2, 2)), dma((2, 2)), dma((2, 4)), dma((2, 4)),
            dma((NZ,)), dma((NZ,)), dma((3,)), dma((3,)),
            dma((NY,)), dma((NY,)), dma((NZ,)), dma((NZ,)), dma((NX,)), dma((NX,)),
        ],
        compiler_params=pltpu.CompilerParams(
            collective_id=0, has_side_effects=True, vmem_limit_bytes=40 * 2**20
        ),
    )(tokens, grad_out, counts, weight, row_state, col_state, jnp.asarray(row_order(), jnp.bfloat16))


def solution(mesh):
    placed = (
        P("dp", None),
        P("dp", "expert"),
        P("dp"),
        P(("expert", "dp"), None),
        P(("expert", "dp")),
        P(),
    )
    return jax.shard_map(
        per_device,
        mesh=mesh,
        in_specs=placed,
        out_specs=(P(("expert", "dp"), None), P(("expert", "dp")), P()),
        check_vma=False,
    )
```

time: 429 us -> 68.3 us (0.16)
  waiting for transfers between devices: 207 us -> 0 us
  blocking collectives: 193 us -> 0 us
  Pallas kernels: 0 us -> 63.4 us
  between operations: 16.8 us -> 1.42 us
  other arithmetic: 4.91 us -> 0 us
    unnamed x2 -> x0, waiting for transfers between devices: 207 us -> none
    psum x2 -> x0, blocking collectives: 193 us -> none  [the longest x1 99.1 us: per_device(): col_total, row_total = lax.psum((col_part, row_part), ('expert', 'dp'))]
    pallas_call x0 -> x1, Pallas kernels: none -> 63.4 us  [per_device(): pl.pallas_call(kernel, out_shape=(jax.ShapeDtypeStruct((OWN, D), jnp.bflo...]
  transfers between devices with their start and end apart: 1 -> 0, of which waited for: 1 -> 0; matrix products, arithmetic and copies ran while one was open for 0% -> 0% of each run, Pallas kernels for 0% -> 0%
where the time goes in v1:
time: 68.3 us; the launch traced here: 68.2 us
  Pallas kernels  63.4 us (93%)
  local copies, waits for them, and re-layouts  3.4 us (5%)
  between operations  1.42 us (2%)
    pallas_call x1, Pallas kernels, per_device(): pl.pallas_call(kernel, out_shape=(jax.ShapeDtypeStruct((OWN, D), jnp.bflo...  63.4 us
    unnamed x14, local copies, waits for them, and re-layouts  3.4 us

profile of v1, /device:TPU:1, one launch (start us, length us, event | category | flops | bytes accessed | tf_op | source)
XLA Modules:
  0.0 68.2 jit_solution(4966464548339399535)
XLA Ops:
  0.6 0.0 copy-start
  0.6 0.0 copy-start.3
  0.7 0.0 copy-start.4
  0.7 0.0 copy-start.2
  0.7 0.0 copy-start.1
  1.4 1.7 %copy.10.tok_ref = bf16[256,2080]{1,0:T(8,128)(2,1)S(1)} copy(bf16[256,2080]{0,1:T(8,128)(2,1)} %param.7) | data formatting | bytes 2129920 | tf_op args[0]
  3.0 0.0 copy-done
  3.0 0.0 copy-done.3
  3.1 0.0 copy-done.4
  3.1 0.0 copy-done.2
  3.1 0.0 copy-done.1
  3.1 63.4 %shard_map.94 = (bf16[6,2080]{1,0:T(8,128)(2,1)S(1)}, f32[6]{0:T(128)S(1)}, f32[2080]{0:T(1024)S(1)}) custom-call(bf16[256,2080]{1,0:T(8,128)(2,1)S(1)} %copy.10.tok_ref, bf16[256,384]{1,0:T(8,128)(2,1)S(1)} %copy-done.1, s32[1]{0:T(128)S(6)} %copy.14.cnt_ref, bf16[6,2080]{1,0:T(8,128)(2,1)S(1)} %copy-done.2, f32[6]{0:T(128)S(1)} %copy-done.4, ...), custom_call_target="tpu_custom_call" | custom-call | tf_op jit(solution)/shard_map/pallas_call | solution.py:247
  66.5 0.6 copy.15
  67.1 0.5 copy.16
  67.6 0.6 copy.17
Async XLA Ops:
  0.6 2.4 %copy-start = (bf16[384,384]{1,0:T(8,128)(2,1)S(1)}, bf16[384,384]{1,0:T(8,128)(2,1)}, u32[]{:S(2)}) copy-start(bf16[384,384]{1,0:T(8,128)(2,1)} %constant.2.clone.pick_ref) | copy-start | bytes 884740
  0.6 2.4 %copy-start.3 = (f32[2080]{0:T(1024)S(1)}, f32[2080]{0:T(1024)}, u32[]{:S(2)}) copy-start(f32[2080]{0:T(1024)} %cs_ref.1) | copy-start | bytes 24964
  0.7 2.4 %copy-start.4 = (f32[6]{0:T(128)S(1)}, f32[6]{0:T(128)}, u32[]{:S(2)}) copy-start(f32[6]{0:T(128)} %rs_ref.1) | copy-start | bytes 76
  0.7 2.4 %copy-start.2 = (bf16[6,2080]{1,0:T(8,128)(2,1)S(1)}, bf16[6,2080]{1,0:T(8,128)(2,1)}, u32[]{:S(2)}) copy-start(bf16[6,2080]{1,0:T(8,128)(2,1)} %w_ref.1) | copy-start | bytes 74884
  0.7 2.4 %copy-start.1 = (bf16[256,384]{1,0:T(8,128)(2,1)S(1)}, bf16[256,384]{1,0:T(8,128)(2,1)}, u32[]{:S(2)}) copy-start(bf16[256,384]{1,0:T(8,128)(2,1)} %go_ref.1) | copy-start | bytes 589828

commit v2 on v0

v2 whole, which is shorter than its diff:
```python
import jax
import jax.numpy as jnp
import numpy as np
from jax import lax
from jax.experimental import pallas as pl
from jax.experimental.pallas import tpu as pltpu
from jax.sharding import PartitionSpec as P

D = 2080
FFW = 3072
NY, NZ, NX = 8, 8, 4
OWN = 6
ROWS = 12
WIDE = 1024
PART = 16
UNIT = (24, 512)
MESH = pl.DeviceIdType.MESH
F32 = jnp.float32
BF16 = jnp.bfloat16


def row_order():
    pick = np.zeros((2, NX, NZ, 24, 384), np.float32)
    tail = np.zeros((NZ, NX, 16, 384), np.float32)
    for x in range(NX):
        for z in range(NZ):
            for k in range(ROWS):
                unit = (z * NX + x) * ROWS + k
                pick[0, x, z, k, unit] = 1
                pick[1, x, z, ROWS + k, unit] = 1
                tail[z, x, k, unit] = 1
    return np.concatenate([pick.reshape(1536, 384), tail.reshape(512, 384)], axis=0)


def kernel(
    tok_ref, go_ref, cnt_ref, w_ref, rs_ref, cs_ref, pick_ref,
    nw_ref, nr_ref, nc_ref,
    lhs, lhs_t, rhs_t, other, acc, core_in, other_t, acc_t, core_t, d2_in, d1_in, z_in, xt_in, zt_in,
    mine_t, g_own, g_sib, gt_own, gt_sib, r_own, r_sib, st_a, st_b, st_f, wide, gwide,
    core_s, core_r, d2_s, d2_r, d1_s, d1_r, zs, zr, xts, xtr, zts, ztr, gs, gr,
    sas, sar, sbs, sbr, sfs, sfr,
):
    e = lax.axis_index("expert")
    q = lax.axis_index("dp")
    c, x, z = q % 2, (q // 2) % NX, q // (2 * NX)

    def at(ee, zz, xx, cc):
        return (ee, (zz * NX + xx) * 2 + cc)

    sib = at(e, z, x, 1 - c)
    y_peers = [at((e + d) % NY, z, x, c) for d in range(1, NY)]
    z_peers = [at(e, (z + d) % NZ, x, c) for d in range(1, NZ)]
    x_peers = [at(e, z, (x + d) % NX, c) for d in range(1, NX)]
    o_peers = [at(e, z, (x + d) % NX, 1 - c) for d in range(1, NX)]
    right, left = x_peers[0], x_peers[2]

    barrier = pltpu.get_barrier_semaphore()
    everyone = [sib] + y_peers + z_peers + x_peers + o_peers
    for peer in everyone:
        pl.semaphore_signal(barrier, inc=1, device_id=peer, device_id_type=MESH)

    def remote(src, dst, s, r, peer):
        return pltpu.make_async_remote_copy(
            src_ref=src, dst_ref=dst, send_sem=s, recv_sem=r, device_id=peer, device_id_type=MESH
        )

    started = []

    def send(*args):
        cp = remote(*args)
        cp.start()
        started.append(cp)
        return cp

    def arrived(buf, sem):
        remote(buf, buf, sem, sem, sib).wait_recv()

    def nt(a, b):
        return lax.dot_general(a, b, (((1,), (1,)), ((), ())), preferred_element_type=F32)

    live = lax.broadcasted_iota(jnp.int32, (256, 384), 0) < cnt_ref[0]
    masked = jnp.where(live, go_ref[...].astype(F32), 0.0).astype(BF16)
    lhs[...] = nt(pick_ref[0:1536, :], masked).astype(BF16).reshape(2, NX, 192, 256)
    picked_t = nt(pick_ref[1536:2048, :], masked).astype(BF16)
    rhs_t[...] = jnp.zeros_like(rhs_t)
    for k in range(NZ):
        lhs_t[:, 256 * k : 256 * (k + 1)] = picked_t[64 * k : 64 * (k + 1)]
        for h in range(2):
            rhs_t[h, PART * k : PART * (k + 1), 256 * k : 256 * (k + 1)] = tok_ref[
                2 * WIDE + PART * h : 2 * WIDE + PART * (h + 1), :
            ]

    def half(k, h):
        first = pl.multiple_of(WIDE * h, WIDE)
        out = nt(lhs[0, k], tok_ref[pl.ds(first, 512), :]) + nt(lhs[1, k], tok_ref[pl.ds(first + 512, 512), :])
        return out.reshape((NZ,) + UNIT)

    def product(k, _):
        other[k] = half(k, 1 - c)
        acc[k] = half(k, c)
        return 0

    lax.fori_loop(0, NX, product, 0)
    other_t[...] = nt(lhs_t[...], rhs_t[1 - c]).reshape(NX, 16, 128)
    acc_t[...] = nt(lhs_t[...], rhs_t[c]).reshape(NX, 16, 128)
    pl.semaphore_wait(barrier, len(everyone))

    slabs = [(x + 2) % NX, (x + 1) % NX, (x + 3) % NX, x]
    core = [send(other.at[k], core_in.at[k], core_s.at[j], core_r.at[j], sib) for j, k in enumerate(slabs)]
    core.append(send(other_t, core_t, core_s.at[4], core_r.at[4], sib))

    def settle(j):
        core[j].wait_recv()
        acc[slabs[j]] += core_in[slabs[j]]

    def zat(d):
        return (z + d) % NZ

    halfway = ((4, 5, 6, 7), (3, 2, 1, 0))
    peer_of = (right, left)

    def skip(side, i):
        k = zat(halfway[side][i])
        send(acc.at[slabs[0], k], d2_in.at[side, i], d2_s.at[side, i], d2_r.at[side, i], peer_of[side])

    def step(side, d):
        k = zat(d)
        if d in halfway[side]:
            i = halfway[side].index(d)
            arrived(d2_in.at[side, i], d2_r.at[side, i])
            acc[slabs[1 + side], k] += d2_in[side, i]
        send(acc.at[slabs[1 + side], k], d1_in.at[side, d], d1_s.at[side, d], d1_r.at[side, d], peer_of[side])

    def deliver(d):
        for side in range(2):
            arrived(d1_in.at[side, d], d1_r.at[side, d])
        acc[x, zat(d)] += d1_in[0, d] + d1_in[1, d]
        if d:
            send(acc.at[x, zat(d)], z_in.at[z], zs.at[d], zr.at[z], z_peers[d - 1])

    settle(0)
    skip(0, 0)
    skip(1, 0)
    skip(0, 1)
    skip(1, 1)
    settle(1)
    settle(2)
    step(0, 3)
    step(1, 4)
    skip(0, 2)
    skip(1, 2)
    settle(3)
    core[4].wait_recv()
    acc_t[...] += core_t[...]
    for d in range(1, NX):
        k = (x + d) % NX
        send(acc_t.at[k], xt_in.at[x], xts.at[d], xtr.at[x], x_peers[d - 1])
    step(0, 4)
    step(1, 3)
    step(0, 5)
    step(1, 2)
    skip(0, 3)
    skip(1, 3)
    step(0, 2)
    step(1, 5)
    deliver(4)
    deliver(3)
    step(0, 6)
    step(1, 1)
    step(0, 1)
    step(1, 6)
    xt = acc_t[x]
    for d in range(1, NX):
        k = (x + d) % NX
        arrived(xt_in.at[k], xtr.at[k])
        xt += xt_in[k]
    mine_t[...] = xt
    for d in range(1, NZ):
        send(mine_t, zt_in.at[z], zts.at[d], ztr.at[z], z_peers[d - 1])
    deliver(5)
    deliver(2)
    step(0, 7)
    step(1, 7)
    step(0, 0)
    step(1, 0)
    deliver(6)
    deliver(1)
    deliver(7)
    deliver(0)
    total = acc[x, z]
    total_t = mine_t[...]
    for d in (4, 5, 3, 6, 2, 7, 1):
        k = zat(d)
        arrived(zt_in.at[k], ztr.at[k])
        total_t += zt_in[k]
        arrived(z_in.at[k], zr.at[k])
        total += z_in[k]

    lane = lax.broadcasted_iota(jnp.int32, (16, 128), 1)
    row = lax.broadcasted_iota(jnp.int32, (16, 128), 0)
    tail = jnp.where((row < ROWS) & (lane // PART == z), total_t, 0.0)
    g_own[...] = total
    gt_own[...] = tail

    squared = total * total
    squared_t = tail * tail
    state = jnp.zeros((16, 128), F32)
    for k in range(OWN):
        state = jnp.where(row == c * OWN + k, rs_ref[k], state)
    sums = jnp.sum(squared, axis=1, keepdims=True)
    sums = sums[0:16] + jnp.concatenate([sums[12:24], sums[0:4]], axis=0) + jnp.sum(squared_t, axis=1, keepdims=True)
    r_own[...] = jnp.where(lane < 64, sums, state)
    r_copy = send(r_own, r_sib, gs.at[0], gr.at[0], sib)
    g_copy = send(g_own, g_sib, gs.at[1], gr.at[1], sib)
    gt_copy = send(gt_own, gt_sib, gs.at[2], gr.at[2], sib)

    row24 = lax.broadcasted_iota(jnp.int32, (24, 1), 0)

    def columns(values, k):
        for h in range(2):
            part = jnp.sum(jnp.where((row24 < ROWS) == (h == 0), values, 0.0), axis=0, keepdims=True)
            for j in range(4):
                st_a[ma, k + 4 * h + j : k + 4 * h + j + 1, :] = part[:, 128 * j : 128 * (j + 1)]

    ma = jnp.where(c == 0, e, z)
    mb = jnp.where(c == 0, z, e)
    columns(squared, 0)
    st_a[ma, 8:9, :] = jnp.sum(squared_t, axis=0, keepdims=True)
    r_copy.wait_recv()
    both = r_own[...] + r_sib[...]
    new_rows = 0.5 * both[:, 64:65] + 0.5 * (both[:, 0:1] / D + 1e-06)
    inverse = 1.0 / new_rows
    columns(squared * jnp.concatenate([inverse[0:12], inverse[0:12]], axis=0), 9)
    st_a[ma, 17:18, :] = jnp.sum(squared_t * inverse, axis=0, keepdims=True)
    row_part = jnp.sum(jnp.where(row[:, 0:1] < ROWS, new_rows, 0.0), axis=0, keepdims=True)
    st_a[ma, 18:24, :] = jnp.broadcast_to(row_part, (6, 128))

    def exchange(buf, me, s, r, peers):
        for d in range(1, 8):
            send(buf.at[me], buf.at[me], s.at[d], r.at[me], peers[d - 1])
        for d in (7, 1, 6, 2, 5, 3, 4):
            k = (me + d) % 8
            arrived(buf.at[k], r.at[k])
        out = buf[0]
        for k in range(1, 8):
            out += buf[k]
        return out

    def either(a, b):
        return tuple(jnp.where(c == 0, i, j) for i, j in zip(a, b))

    st_b[mb] = exchange(st_a, ma, sas, sar, [either(a, b) for a, b in zip(y_peers, z_peers)])
    st_f[c, x] = exchange(st_b, mb, sbs, sbr, [either(b, a) for a, b in zip(y_peers, z_peers)])
    send(st_f.at[c, x], st_f.at[c, x], sfs.at[6], sfr.at[c, x], sib)
    for d in range(1, NX):
        send(st_f.at[c, x], st_f.at[c, x], sfs.at[d - 1], sfr.at[c, x], x_peers[d - 1])
        send(st_f.at[c, x], st_f.at[c, x], sfs.at[d + 2], sfr.at[c, x], o_peers[d - 1])

    def halves(own, sibling):
        return jnp.where(c == 0, own, sibling), jnp.where(c == 0, sibling, own)

    def fold(v):
        for shift in (64, 32, 16):
            v = v + pltpu.roll(v, shift, 1)
        return v

    def rows_of(v, first):
        return jnp.where(c == 0, v[first : first + 6], v[first + 6 : first + 12])

    g_copy.wait_recv()
    gt_copy.wait_recv()
    low, high = halves(g_own[...], g_sib[...])
    for h in range(2):
        gwide[0:OWN, 512 * h : 512 * (h + 1)] = rows_of(low, ROWS * h)
        gwide[0:OWN, WIDE + 512 * h : WIDE + 512 * (h + 1)] = rows_of(high, ROWS * h)
    low, high = halves(fold(gt_own[...]), fold(gt_sib[...]))
    gwide[0:OWN, 2 * WIDE :] = rows_of(jnp.where(lane < PART, low, high), 0)
    rows6 = rows_of(new_rows, 0)
    eye = lax.broadcasted_iota(jnp.int32, (OWN, 128), 0) == lax.broadcasted_iota(jnp.int32, (OWN, 128), 1)
    nr_ref[...] = jnp.sum(jnp.where(eye, rows6, 0.0), axis=0)[0:OWN]

    arrived(st_f.at[1 - c, x], sfr.at[1 - c, x])
    for d in range(1, NX):
        for cc in range(2):
            k = (x + d) % NX
            core_k = (c + cc) % 2
            arrived(st_f.at[core_k, k], sfr.at[core_k, k])
    sums = []
    for cc in range(2):
        v = st_f[cc, 0]
        for k in range(1, NX):
            v += st_f[cc, k]
        sums.append(v)
    for cc in range(2):
        for j in range(2):
            for k in range(8):
                first = WIDE * cc + 128 * k
                wide[j : j + 1, first : first + 128] = sums[cc][9 * j + k : 9 * j + k + 1]
    for j in range(2):
        low, high = (fold(v[9 * j + 8 : 9 * j + 9]) for v in sums)
        wide[j : j + 1, 2 * WIDE :] = jnp.where(lane[0:1] < PART, low, high)
    row_avg = sums[0][18:19, 0:1] / FFW
    new_cols = 0.5 * cs_ref[...].reshape(1, D) + 0.5 * (wide[0:1, 0:D] / FFW + 1e-06)
    nc_ref[...] = new_cols.reshape(D)
    total_sq = row_avg * jnp.sum(wide[1:2, 0:D] / new_cols, axis=1, keepdims=True)
    rms = jnp.sqrt(total_sq / (FFW * D))
    factor = 0.1 / jnp.maximum(1.0, rms) * jnp.sqrt(row_avg)
    scaled = gwide[0:OWN, 0:D] * (lax.rsqrt(rows6) * factor) * lax.rsqrt(new_cols)
    nw_ref[...] = (w_ref[...].astype(F32) - scaled).astype(BF16)

    for cp in started:
        cp.wait_send()


def per_device(tokens, grad_out, counts, weight, row_state, col_state):
    vmem = pl.BlockSpec(memory_space=pltpu.VMEM)
    smem = pl.BlockSpec(memory_space=pltpu.SMEM)
    dma = pltpu.SemaphoreType.DMA

    def f32(*shape):
        return pltpu.VMEM(shape, F32)

    return pl.pallas_call(
        kernel,
        out_shape=(
            jax.ShapeDtypeStruct((OWN, D), BF16),
            jax.ShapeDtypeStruct((OWN,), F32),
            jax.ShapeDtypeStruct((D,), F32),
        ),
        in_specs=[vmem, vmem, smem, vmem, smem, vmem, vmem],
        out_specs=(vmem, vmem, vmem),
        scratch_shapes=[
            pltpu.VMEM((2, NX, 192, 256), BF16),
            pltpu.VMEM((64, 2048), BF16),
            pltpu.VMEM((2, 128, 2048), BF16),
            f32(NX, NZ, *UNIT), f32(NX, NZ, *UNIT), f32(NX, NZ, *UNIT),
            f32(NX, 16, 128), f32(NX, 16, 128), f32(NX, 16, 128),
            f32(2, 4, *UNIT), f32(2, NZ, *UNIT), f32(NZ, *UNIT),
            f32(NX, 16, 128), f32(NZ, 16, 128), f32(16, 128),
            f32(*UNIT), f32(*UNIT), f32(16, 128), f32(16, 128), f32(16, 128), f32(16, 128),
            f32(8, 24, 128), f32(8, 24, 128), f32(2, NX, 24, 128),
            f32(8, 2 * WIDE + 128), f32(8, 2 * WIDE + 128),
            dma((5,)), dma((5,)), dma((2, 4)), dma((2, 4)), dma((2, NZ)), dma((2, NZ)),
            dma((NZ,)), dma((NZ,)), dma((NX,)), dma((NX,)), dma((NZ,)), dma((NZ,)), dma((3,)), dma((3,)),
            dma((8,)), dma((8,)), dma((8,)), dma((8,)), dma((7,)), dma((2, NX)),
        ],
        compiler_params=pltpu.CompilerParams(
            collective_id=0, has_side_effects=True, vmem_limit_bytes=40 * 2**20
        ),
    )(tokens.T, grad_out, counts, weight, row_state, col_state, jnp.asarray(row_order(), BF16))


def solution(mesh):
    placed = (
        P("dp", None),
        P("dp", "expert"),
        P("dp"),
        P(("expert", "dp"), None),
        P(("expert", "dp")),
        P(),
    )
    return jax.shard_map(
        per_device,
        mesh=mesh,
        in_specs=placed,
        out_specs=(P(("expert", "dp"), None), P(("expert", "dp")), P()),
        check_vma=False,
    )
```

time: 429 us -> 64.9 us (0.15)
  waiting for transfers between devices: 207 us -> 0 us
  blocking collectives: 193 us -> 0 us
  Pallas kernels: 0 us -> 55.9 us
  between operations: 16.8 us -> 1.3 us
  local copies, waits for them, and re-layouts: 1.75 us -> 7.41 us
  other arithmetic: 4.91 us -> 0 us
    unnamed x2 -> x0, waiting for transfers between devices: 207 us -> none
    psum x2 -> x0, blocking collectives: 193 us -> none  [the longest x1 99.1 us: per_device(): col_total, row_total = lax.psum((col_part, row_part), ('expert', 'dp'))]
    pallas_call x0 -> x1, Pallas kernels: none -> 55.9 us  [per_device(): pl.pallas_call(kernel, out_shape=(jax.ShapeDtypeStruct((OWN, D), BF16), j...]
    unnamed x13 -> x15, local copies, waits for them, and re-layouts: 1.75 us -> 7.41 us
  transfers between devices with their start and end apart: 1 -> 0, of which waited for: 1 -> 0; matrix products, arithmetic and copies ran while one was open for 0% -> 0% of each run, Pallas kernels for 0% -> 0%
where the time goes in v2:
time: 64.9 us; the launch traced here: 64.6 us
  Pallas kernels  55.9 us (86%)
  local copies, waits for them, and re-layouts  7.41 us (11%)
  between operations  1.3 us (2%)
    pallas_call x1, Pallas kernels, per_device(): pl.pallas_call(kernel, out_shape=(jax.ShapeDtypeStruct((OWN, D), BF16), j...  55.9 us
    unnamed x15, local copies, waits for them, and re-layouts  7.41 us

profile of v2, /device:TPU:1, one launch (start us, length us, event | category | flops | bytes accessed | tf_op | source)
XLA Modules:
  0.0 64.6 jit_solution(12633922096370116756)
XLA Ops:
  1.3 0.0 copy-start
  1.3 1.4 %copy-done = bf16[2048,384]{1,0:T(8,128)(2,1)S(1)} copy-done((bf16[2048,384]{1,0:T(8,128)(2,1)S(1)}, bf16[2048,384]{1,0:T(8,128)(2,1)}, u32[]{:S(2)}) %copy-start) | copy-done | bytes 1572888
  2.7 0.0 copy-start.1
  2.7 1.2 %copy-done.1 = bf16[256,2080]{0,1:T(8,128)(2,1)S(1)} copy-done((bf16[256,2080]{0,1:T(8,128)(2,1)S(1)}, bf16[256,2080]{0,1:T(8,128)(2,1)}, u32[]{:S(2)}) %copy-start.1) | copy-done | bytes 1064984
  3.9 0.0 copy-start.2
  3.9 0.9 %copy-done.2 = bf16[256,384]{1,0:T(8,128)(2,1)S(1)} copy-done((bf16[256,384]{1,0:T(8,128)(2,1)S(1)}, bf16[256,384]{1,0:T(8,128)(2,1)}, u32[]{:S(2)}) %copy-start.2) | copy-done | bytes 196632
  4.8 0.0 copy-start.3
  4.8 0.8 %copy-done.3 = bf16[6,2080]{1,0:T(8,128)(2,1)S(1)} copy-done((bf16[6,2080]{1,0:T(8,128)(2,1)S(1)}, bf16[6,2080]{1,0:T(8,128)(2,1)}, u32[]{:S(2)}) %copy-start.3) | copy-done | bytes 24984
  5.6 0.0 copy-start.4
  5.6 0.7 %copy-done.4 = f32[2080]{0:T(1024)S(1)} copy-done((f32[2080]{0:T(1024)S(1)}, f32[2080]{0:T(1024)}, u32[]{:S(2)}) %copy-start.4) | copy-done | bytes 8344
  6.3 0.0 copy-start.5
  6.3 0.7 %copy-done.5 = f32[6]{0:T(128)S(1)} copy-done((f32[6]{0:T(128)S(1)}, f32[6]{0:T(128)}, u32[]{:S(2)}) %copy-start.5) | copy-done | bytes 48
  7.0 55.9 %shard_map.94 = (bf16[6,2080]{1,0:T(8,128)(2,1)S(1)}, f32[6]{0:T(128)S(1)}, f32[2080]{0:T(1024)S(1)}) custom-call(bf16[2080,256]{1,0:T(8,128)(2,1)S(1)} %bitcast.1, bf16[256,384]{1,0:T(8,128)(2,1)S(1)} %copy-done.2, s32[1]{0:T(128)S(6)} %copy.13.cnt_ref, bf16[6,2080]{1,0:T(8,128)(2,1)S(1)} %copy-done.3, f32[6]{0:T(128)S(1)} %copy-done.5, ...), custom_call_target="tpu_custom_call" | custom-call | tf_op jit(solution)/shard_map/pallas_call | solution.py:323
  62.9 0.6 copy.14
  63.5 0.5 copy.15
  64.0 0.6 copy.16
Async XLA Ops:
  1.3 1.4 %copy-start = (bf16[2048,384]{1,0:T(8,128)(2,1)S(1)}, bf16[2048,384]{1,0:T(8,128)(2,1)}, u32[]{:S(2)}) copy-start(bf16[2048,384]{1,0:T(8,128)(2,1)} %constant.2.clone.pick_ref) | copy-start | bytes 4718596
  2.7 1.2 %copy-start.1 = (bf16[256,2080]{0,1:T(8,128)(2,1)S(1)}, bf16[256,2080]{0,1:T(8,128)(2,1)}, u32[]{:S(2)}) copy-start(bf16[256,2080]{0,1:T(8,128)(2,1)} %param.7) | copy-start | bytes 3194884
  3.9 0.9 %copy-start.2 = (bf16[256,384]{1,0:T(8,128)(2,1)S(1)}, bf16[256,384]{1,0:T(8,128)(2,1)}, u32[]{:S(2)}) copy-start(bf16[256,384]{1,0:T(8,128)(2,1)} %go_ref.1) | copy-start | bytes 589828
  4.8 0.8 %copy-start.3 = (bf16[6,2080]{1,0:T(8,128)(2,1)S(1)}, bf16[6,2080]{1,0:T(8,128)(2,1)}, u32[]{:S(2)}) copy-start(bf16[6,2080]{1,0:T(8,128)(2,1)} %w_ref.1) | copy-start | bytes 74884
  5.6 0.7 %copy-start.4 = (f32[2080]{0:T(1024)S(1)}, f32[2080]{0:T(1024)}, u32[]{:S(2)}) copy-start(f32[2080]{0:T(1024)} %cs_ref.1) | copy-start | bytes 24964
  6.3 0.7 %copy-start.5 = (f32[6]{0:T(128)S(1)}, f32[6]{0:T(128)}, u32[]{:S(2)}) copy-start(f32[6]{0:T(128)} %rs_ref.1) | copy-start | bytes 76

commit v3 on v2

--- a/solution.py
+++ b/solution.py
@@ -1,6 +1,5 @@
 import jax
 import jax.numpy as jnp
-import numpy as np
 from jax import lax
 from jax.experimental import pallas as pl
 from jax.experimental.pallas import tpu as pltpu
@@ -19,25 +18,12 @@
 BF16 = jnp.bfloat16
 
 
-def row_order():
-    pick = np.zeros((2, NX, NZ, 24, 384), np.float32)
-    tail = np.zeros((NZ, NX, 16, 384), np.float32)
-    for x in range(NX):
-        for z in range(NZ):
-            for k in range(ROWS):
-                unit = (z * NX + x) * ROWS + k
-                pick[0, x, z, k, unit] = 1
-                pick[1, x, z, ROWS + k, unit] = 1
-                tail[z, x, k, unit] = 1
-    return np.concatenate([pick.reshape(1536, 384), tail.reshape(512, 384)], axis=0)
-
-
 def kernel(
-    tok_ref, go_ref, cnt_ref, w_ref, rs_ref, cs_ref, pick_ref,
+    tok_hbm, go_hbm, cnt_hbm, w_hbm, rs_hbm, cs_hbm,
     nw_ref, nr_ref, nc_ref,
-    lhs, lhs_t, rhs_t, other, acc, core_in, other_t, acc_t, core_t, d2_in, d1_in, z_in, xt_in, zt_in,
+    tok_ref, go_ref, cnt_ref, w_ref, rs_ref, cs_ref, in_s, lhs, picked_t, lhs_t, rhs_t, other, acc, core_in, other_t, acc_t, core_t, d2_in, d1_in, z_in, xt_in, zt_in,
     mine_t, g_own, g_sib, gt_own, gt_sib, r_own, r_sib, st_a, st_b, st_f, wide, gwide,
-    core_s, core_r, d2_s, d2_r, d1_s, d1_r, zs, zr, xts, xtr, zts, ztr, gs, gr,
+    first_s, first_r, core_s, core_r, d2_s, d2_r, d1_s, d1_r, zs, zr, xts, xtr, zts, ztr, gs, gr,
     sas, sar, sbs, sbr, sfs, sfr,
 ):
     e = lax.axis_index("expert")
@@ -54,6 +40,14 @@
     o_peers = [at(e, z, (x + d) % NX, 1 - c) for d in range(1, NX)]
     right, left = x_peers[0], x_peers[2]
 
+    loads = [
+        pltpu.make_async_copy(src, dst, in_s.at[k])
+        for k, (src, dst) in enumerate(
+            [(cnt_hbm, cnt_ref), (go_hbm, go_ref), (tok_hbm, tok_ref), (rs_hbm, rs_ref), (cs_hbm, cs_ref), (w_hbm, w_ref)]
+        )
+    ]
+    for cp in loads:
+        cp.start()
     barrier = pltpu.get_barrier_semaphore()
     everyone = [sib] + y_peers + z_peers + x_peers + o_peers
     for peer in everyone:
@@ -78,49 +72,54 @@
     def nt(a, b):
         return lax.dot_general(a, b, (((1,), (1,)), ((), ())), preferred_element_type=F32)
 
+    row = lax.broadcasted_iota(jnp.int32, (512, 384), 0)
+    k = row & 15
+    unit = ((row >> 4) & 7) * (NX * ROWS) + (row >> 7) * ROWS + k
+    pick = (lax.broadcasted_iota(jnp.int32, (512, 384), 1) == unit) & (k < ROWS)
+    pick = jnp.where(pick, 1.0, 0.0).astype(BF16)
+    loads[0].wait()
+    loads[1].wait()
     live = lax.broadcasted_iota(jnp.int32, (256, 384), 0) < cnt_ref[0]
     masked = jnp.where(live, go_ref[...].astype(F32), 0.0).astype(BF16)
-    lhs[...] = nt(pick_ref[0:1536, :], masked).astype(BF16).reshape(2, NX, 192, 256)
-    picked_t = nt(pick_ref[1536:2048, :], masked).astype(BF16)
-    rhs_t[...] = jnp.zeros_like(rhs_t)
-    for k in range(NZ):
-        lhs_t[:, 256 * k : 256 * (k + 1)] = picked_t[64 * k : 64 * (k + 1)]
-        for h in range(2):
-            rhs_t[h, PART * k : PART * (k + 1), 256 * k : 256 * (k + 1)] = tok_ref[
-                2 * WIDE + PART * h : 2 * WIDE + PART * (h + 1), :
-            ]
+    picked = nt(pick, masked)
+    picked_t[...] = picked.astype(BF16).reshape(NX, 128, 256)
+    units = picked.reshape(NX * NZ, 16, 256)
+    blank = jnp.zeros((NX * NZ, 8, 256), F32)
+    lhs[0] = jnp.concatenate([units, blank], axis=1).reshape(768, 256).astype(BF16).reshape(NX, 192, 256)
+    moved = jnp.concatenate([blank, pltpu.roll(units, 4, 1)], axis=1)
+    lhs[1] = moved.reshape(768, 256).astype(BF16).reshape(NX, 192, 256)
 
     def half(k, h):
         first = pl.multiple_of(WIDE * h, WIDE)
         out = nt(lhs[0, k], tok_ref[pl.ds(first, 512), :]) + nt(lhs[1, k], tok_ref[pl.ds(first + 512, 512), :])
         return out.reshape((NZ,) + UNIT)
 
-    def product(k, _):
-        other[k] = half(k, 1 - c)
-        acc[k] = half(k, c)
-        return 0
-
-    lax.fori_loop(0, NX, product, 0)
-    other_t[...] = nt(lhs_t[...], rhs_t[1 - c]).reshape(NX, 16, 128)
-    acc_t[...] = nt(lhs_t[...], rhs_t[c]).reshape(NX, 16, 128)
-    pl.semaphore_wait(barrier, len(everyone))
-
+    loads[2].wait()
     slabs = [(x + 2) % NX, (x + 1) % NX, (x + 3) % NX, x]
-    core = [send(other.at[k], core_in.at[k], core_s.at[j], core_r.at[j], sib) for j, k in enumerate(slabs)]
-    core.append(send(other_t, core_t, core_s.at[4], core_r.at[4], sib))
-
-    def settle(j):
-        core[j].wait_recv()
-        acc[slabs[j]] += core_in[slabs[j]]
 
     def zat(d):
         return (z + d) % NZ
 
+    def offer(j):
+        k = slabs[j]
+        other[k] = half(k, 1 - c)
+        send(other.at[k], core_in.at[k], core_s.at[j], core_r.at[j], sib)
+
+    def settle(j):
+        k = slabs[j]
+        arrived(core_in.at[k], core_r.at[j])
+        acc[k] += core_in[k]
+
+    def own(j):
+        acc[slabs[j]] = half(slabs[j], c)
+
     halfway = ((4, 5, 6, 7), (3, 2, 1, 0))
     peer_of = (right, left)
 
     def skip(side, i):
         k = zat(halfway[side][i])
+        arrived(core_in.at[slabs[0], k], first_r.at[4 * side + i])
+        acc[slabs[0], k] += core_in[slabs[0], k]
         send(acc.at[slabs[0], k], d2_in.at[side, i], d2_s.at[side, i], d2_r.at[side, i], peer_of[side])
 
     def step(side, d):
@@ -138,27 +137,47 @@
         if d:
             send(acc.at[x, zat(d)], z_in.at[z], zs.at[d], zr.at[z], z_peers[d - 1])
 
-    settle(0)
-    skip(0, 0)
-    skip(1, 0)
-    skip(0, 1)
-    skip(1, 1)
+    other[slabs[0]] = half(slabs[0], 1 - c)
+    pl.semaphore_wait(barrier, len(everyone))
+    for i in range(4):
+        for side in range(2):
+            k, j = zat(halfway[side][i]), 4 * side + i
+            send(other.at[slabs[0], k], core_in.at[slabs[0], k], first_s.at[j], first_r.at[j], sib)
+    own(0)
+    for i in range(3):
+        skip(0, i)
+        skip(1, i)
+    offer(1)
+    offer(2)
+    own(1)
     settle(1)
+    step(0, 3)
+    own(2)
     settle(2)
-    step(0, 3)
     step(1, 4)
-    skip(0, 2)
-    skip(1, 2)
+    step(0, 4)
+    step(1, 3)
+    offer(3)
+    rhs_t[...] = jnp.zeros_like(rhs_t)
+    for k in range(NZ):
+        for j in range(NX):
+            lhs_t[16 * j : 16 * (j + 1), 256 * k : 256 * (k + 1)] = picked_t[j, 16 * k : 16 * (k + 1), :]
+        for h in range(2):
+            rhs_t[h, PART * k : PART * (k + 1), 256 * k : 256 * (k + 1)] = tok_ref[
+                2 * WIDE + PART * h : 2 * WIDE + PART * (h + 1), :
+            ]
+    other_t[...] = nt(lhs_t[...], rhs_t[1 - c]).reshape(NX, 16, 128)
+    send(other_t, core_t, core_s.at[0], core_r.at[0], sib)
+    acc_t[...] = nt(lhs_t[...], rhs_t[c]).reshape(NX, 16, 128)
+    own(3)
     settle(3)
-    core[4].wait_recv()
+    step(0, 5)
+    step(1, 2)
+    arrived(core_t, core_r.at[0])
     acc_t[...] += core_t[...]
     for d in range(1, NX):
         k = (x + d) % NX
         send(acc_t.at[k], xt_in.at[x], xts.at[d], xtr.at[x], x_peers[d - 1])
-    step(0, 4)
-    step(1, 3)
-    step(0, 5)
-    step(1, 2)
     skip(0, 3)
     skip(1, 3)
     step(0, 2)
@@ -202,6 +221,8 @@
     g_own[...] = total
     gt_own[...] = tail
 
+    for cp in loads[3:]:
+        cp.wait()
     squared = total * total
     squared_t = tail * tail
     state = jnp.zeros((16, 128), F32)
@@ -312,25 +333,37 @@
         cp.wait_send()
 
 
+def store(a, b, c, a_out, b_out, c_out, sem):
+    copies = [pltpu.make_async_copy(src, dst, sem.at[k]) for k, (src, dst) in enumerate([(a, a_out), (b, b_out), (c, c_out)])]
+    for cp in copies:
+        cp.start()
+    for cp in copies:
+        cp.wait()
+
+
 def per_device(tokens, grad_out, counts, weight, row_state, col_state):
     vmem = pl.BlockSpec(memory_space=pltpu.VMEM)
-    smem = pl.BlockSpec(memory_space=pltpu.SMEM)
     dma = pltpu.SemaphoreType.DMA
 
     def f32(*shape):
         return pltpu.VMEM(shape, F32)
 
-    return pl.pallas_call(
+    hbm = pl.BlockSpec(memory_space=pltpu.MemorySpace.HBM)
+    results = (
+        jax.ShapeDtypeStruct((OWN, D), BF16),
+        jax.ShapeDtypeStruct((OWN,), F32),
+        jax.ShapeDtypeStruct((D,), F32),
+    )
+    computed = pl.pallas_call(
         kernel,
-        out_shape=(
-            jax.ShapeDtypeStruct((OWN, D), BF16),
-            jax.ShapeDtypeStruct((OWN,), F32),
-            jax.ShapeDtypeStruct((D,), F32),
-        ),
-        in_specs=[vmem, vmem, smem, vmem, smem, vmem, vmem],
+        out_shape=tuple(pltpu.VMEM(r.shape, r.dtype) for r in results),
+        in_specs=[hbm] * 6,
         out_specs=(vmem, vmem, vmem),
         scratch_shapes=[
+            pltpu.VMEM((D, 256), BF16), pltpu.VMEM((256, 384), BF16), pltpu.SMEM((1,), jnp.int32),
+            pltpu.VMEM((OWN, D), BF16), pltpu.SMEM((OWN,), F32), pltpu.VMEM((D,), F32), dma((6,)),
             pltpu.VMEM((2, NX, 192, 256), BF16),
+            pltpu.VMEM((NX, 128, 256), BF16),
             pltpu.VMEM((64, 2048), BF16),
             pltpu.VMEM((2, 128, 2048), BF16),
             f32(NX, NZ, *UNIT), f32(NX, NZ, *UNIT), f32(NX, NZ, *UNIT),
@@ -340,14 +373,21 @@
             f32(*UNIT), f32(*UNIT), f32(16, 128), f32(16, 128), f32(16, 128), f32(16, 128),
             f32(8, 24, 128), f32(8, 24, 128), f32(2, NX, 24, 128),
             f32(8, 2 * WIDE + 128), f32(8, 2 * WIDE + 128),
-            dma((5,)), dma((5,)), dma((2, 4)), dma((2, 4)), dma((2, NZ)), dma((2, NZ)),
+            dma((8,)), dma((8,)), dma((4,)), dma((4,)), dma((2, 4)), dma((2, 4)), dma((2, NZ)), dma((2, NZ)),
             dma((NZ,)), dma((NZ,)), dma((NX,)), dma((NX,)), dma((NZ,)), dma((NZ,)), dma((3,)), dma((3,)),
             dma((8,)), dma((8,)), dma((8,)), dma((8,)), dma((7,)), dma((2, NX)),
         ],
         compiler_params=pltpu.CompilerParams(
-            collective_id=0, has_side_effects=True, vmem_limit_bytes=40 * 2**20
+            collective_id=0, has_side_effects=True, vmem_limit_bytes=56 * 2**20
         ),
-    )(tokens.T, grad_out, counts, weight, row_state, col_state, jnp.asarray(row_order(), BF16))
+    )(tokens.T, grad_out, counts, weight, row_state, col_state)
+    return pl.pallas_call(
+        store,
+        out_shape=results,
+        in_specs=[vmem] * 3,
+        out_specs=(hbm, hbm, hbm),
+        scratch_shapes=[dma((3,))],
+    )(*computed)
 
 
 def solution(mesh):

time: 64.9 us -> 58.7 us (0.904)
  local copies, waits for them, and re-layouts: 7.41 us -> 1.7 us
    unnamed x15 -> x6, local copies, waits for them, and re-layouts: 7.41 us -> 1.7 us
    pallas_call x1 -> x2, Pallas kernels: 55.9 us -> 55.4 us  [the longest x1 54 us: per_device(): pl.pallas_call(kernel, out_shape=tuple((pltpu.VMEM(r.shape, r.dtype) for...]
where the time goes in v3:
time: 58.7 us; the launch traced here: 58.4 us
  Pallas kernels  55.4 us (94%)
  local copies, waits for them, and re-layouts  1.7 us (3%)
  between operations  1.3 us (2%)
    pallas_call x1, Pallas kernels, per_device(): pl.pallas_call(kernel, out_shape=tuple((pltpu.VMEM(r.shape, r.dtype) for...  54 us
    unnamed x6, local copies, waits for them, and re-layouts  1.7 us
    pallas_call x1, Pallas kernels, per_device(): pl.pallas_call(store, out_shape=results, in_specs=[vmem] * 3, out_specs=(...  1.41 us

profile of v3, /device:TPU:1, one launch (start us, length us, event | category | flops | bytes accessed | tf_op | source)
XLA Modules:
  0.0 58.4 jit_solution(15142506422248173050)
XLA Ops:
  1.3 54.0 %shard_map.85 = (bf16[6,2080]{1,0:T(8,128)(2,1)S(1)}, f32[6]{0:T(128)S(1)}, f32[2080]{0:T(1024)S(1)}) custom-call(bf16[2080,256]{1,0:T(8,128)(2,1)} %bitcast.1, bf16[256,384]{1,0:T(8,128)(2,1)} %go_hbm.1, s32[1]{0:T(128)S(6)} %copy.9.cnt_hbm, bf16[6,2080]{1,0:T(8,128)(2,1)} %w_hbm.1, f32[6]{0:T(128)} %rs_hbm.1, f32[2080]{0:T(1024)} %cs_hbm.1), custom_call_target="tpu_custom_call" | custom-call | tf_op jit(solution)/shard_map/pallas_call | solution.py:357
  55.3 0.0 copy-start
  55.3 0.6 %copy-done = bf16[6,2080]{1,0:T(8,128)(2,1)} copy-done((bf16[6,2080]{1,0:T(8,128)(2,1)}, bf16[6,2080]{1,0:T(8,128)(2,1)S(1)}, u32[]{:S(2)}) %copy-start) | copy-done | bytes 24984
  55.9 0.0 copy-start.1
  55.9 0.6 %copy-done.1 = f32[2080]{0:T(1024)} copy-done((f32[2080]{0:T(1024)}, f32[2080]{0:T(1024)S(1)}, u32[]{:S(2)}) %copy-start.1) | copy-done | bytes 8344
  56.5 0.0 copy-start.2
  56.5 0.5 copy-done.2
  57.0 1.4 %shard_map.86 = (bf16[6,2080]{1,0:T(8,128)(2,1)}, f32[6]{0:T(128)}, f32[2080]{0:T(1024)}) custom-call(bf16[6,2080]{1,0:T(8,128)(2,1)} %copy-done, f32[6]{0:T(128)} %copy-done.2, f32[2080]{0:T(1024)} %copy-done.1), custom_call_target="tpu_custom_call" | custom-call | tf_op jit(solution)/shard_map/pallas_call | solution.py:384
Async XLA Ops:
  55.3 0.6 %copy-start = (bf16[6,2080]{1,0:T(8,128)(2,1)}, bf16[6,2080]{1,0:T(8,128)(2,1)S(1)}, u32[]{:S(2)}) copy-start(bf16[6,2080]{1,0:T(8,128)(2,1)S(1)} %get-tuple-element.6.a) | copy-start | bytes 74884
  55.9 0.6 %copy-start.1 = (f32[2080]{0:T(1024)}, f32[2080]{0:T(1024)S(1)}, u32[]{:S(2)}) copy-start(f32[2080]{0:T(1024)S(1)} %get-tuple-element.8.c) | copy-start | bytes 24964
  56.5 0.5 copy-start.2

commit v4 on v3

--- a/solution.py
+++ b/solution.py
@@ -257,8 +257,12 @@
     st_a[ma, 18:24, :] = jnp.broadcast_to(row_part, (6, 128))
 
     def exchange(buf, me, s, r, peers):
+        done = list(started)
         for d in range(1, 8):
             send(buf.at[me], buf.at[me], s.at[d], r.at[me], peers[d - 1])
+        for cp in done:
+            cp.wait_send()
+            started.remove(cp)
         for d in (7, 1, 6, 2, 5, 3, 4):
             k = (me + d) % 8
             arrived(buf.at[k], r.at[k])
@@ -272,10 +276,15 @@
 
     st_b[mb] = exchange(st_a, ma, sas, sar, [either(a, b) for a, b in zip(y_peers, z_peers)])
     st_f[c, x] = exchange(st_b, mb, sbs, sbr, [either(b, a) for a, b in zip(y_peers, z_peers)])
+    done = list(started)
+    started.clear()
     send(st_f.at[c, x], st_f.at[c, x], sfs.at[6], sfr.at[c, x], sib)
     for d in range(1, NX):
         send(st_f.at[c, x], st_f.at[c, x], sfs.at[d - 1], sfr.at[c, x], x_peers[d - 1])
         send(st_f.at[c, x], st_f.at[c, x], sfs.at[d + 2], sfr.at[c, x], o_peers[d - 1])
+
+    for cp in done:
+        cp.wait_send()
 
     def halves(own, sibling):
         return jnp.where(c == 0, own, sibling), jnp.where(c == 0, sibling, own)
@@ -387,6 +396,7 @@
         in_specs=[vmem] * 3,
         out_specs=(hbm, hbm, hbm),
         scratch_shapes=[dma((3,))],
+        compiler_params=pltpu.CompilerParams(vmem_limit_bytes=2**20),
     )(*computed)
 
 

time: 58.7 us -> 56 us (0.954)
  local copies, waits for them, and re-layouts: 1.7 us -> 0 us
  Pallas kernels: 55.4 us -> 54.6 us
    unnamed x6 -> x0, local copies, waits for them, and re-layouts: 1.7 us -> none
    pallas_call x1, Pallas kernels: 1.41 us -> 0.65 us  [per_device(): pl.pallas_call(store, out_shape=results, in_specs=[vmem] * 3, out_specs=(...]
where the time goes in v4:
time: 56 us; the launch traced here: 55.8 us
  Pallas kernels  54.6 us (98%)
  between operations  1.28 us (2%)
    pallas_call x1, Pallas kernels, per_device(): pl.pallas_call(kernel, out_shape=tuple((pltpu.VMEM(r.shape, r.dtype) for...  53.9 us

profile of v4, /device:TPU:1, one launch (start us, length us, event | category | flops | bytes accessed | tf_op | source)
XLA Modules:
  0.0 55.8 jit_solution(901229854426432226)
XLA Ops:
  1.3 53.9 %shard_map.85 = (bf16[6,2080]{1,0:T(8,128)(2,1)S(1)}, f32[6]{0:T(128)S(1)}, f32[2080]{0:T(1024)S(1)}) custom-call(bf16[2080,256]{1,0:T(8,128)(2,1)} %bitcast.1, bf16[256,384]{1,0:T(8,128)(2,1)} %go_hbm.1, s32[1]{0:T(128)S(6)} %copy.9.cnt_hbm, bf16[6,2080]{1,0:T(8,128)(2,1)} %w_hbm.1, f32[6]{0:T(128)} %rs_hbm.1, f32[2080]{0:T(1024)} %cs_hbm.1), custom_call_target="tpu_custom_call" | custom-call | tf_op jit(solution)/shard_map/pallas_call | solution.py:366
  55.2 0.6 %shard_map.86 = (bf16[6,2080]{1,0:T(8,128)(2,1)}, f32[6]{0:T(128)}, f32[2080]{0:T(1024)}) custom-call(bf16[6,2080]{1,0:T(8,128)(2,1)S(1)} %get-tuple-element.6.a, f32[6]{0:T(128)S(1)} %get-tuple-element.7.b, f32[2080]{0:T(1024)S(1)} %get-tuple-element.8.c), custom_call_target="tpu_custom_call" | custom-call | tf_op jit(solution)/shard_map/pallas_call | solution.py:393

commit v5 on v4

--- a/solution.py
+++ b/solution.py
@@ -12,6 +12,7 @@
 ROWS = 12
 WIDE = 1024
 PART = 16
+MAIN = 384
 UNIT = (24, 512)
 MESH = pl.DeviceIdType.MESH
 F32 = jnp.float32
@@ -21,9 +22,9 @@
 def kernel(
     tok_hbm, go_hbm, cnt_hbm, w_hbm, rs_hbm, cs_hbm,
     nw_ref, nr_ref, nc_ref,
-    tok_ref, go_ref, cnt_ref, w_ref, rs_ref, cs_ref, in_s, lhs, picked_t, lhs_t, rhs_t, other, acc, core_in, other_t, acc_t, core_t, d2_in, d1_in, z_in, xt_in, zt_in,
+    tok_ref, go_ref, cnt_ref, w_ref, rs_ref, cs_ref, in_s, lhs, picked_t, lhs_t, rhs_t, other, acc, core_in, other_b, acc_b, core_b, bz_in, bm_in, bx_in, other_t, acc_t, core_t, d2_in, d1_in, z_in, zm_in, xt_in, zt_in,
     mine_t, g_own, g_sib, gt_own, gt_sib, r_own, r_sib, st_a, st_b, st_f, wide, gwide,
-    first_s, first_r, core_s, core_r, d2_s, d2_r, d1_s, d1_r, zs, zr, xts, xtr, zts, ztr, gs, gr,
+    first_s, first_r, bc_s, bc_r, bz_s, bz_r, bm_s, bm_r, bx_s, bx_r, core_s, core_r, d2_s, d2_r, d1_s, d1_r, zs, zr, zms, zmr, xts, xtr, zts, ztr, gs, gr,
     sas, sar, sbs, sbr, sfs, sfr,
 ):
     e = lax.axis_index("expert")
@@ -91,8 +92,15 @@
 
     def half(k, h):
         first = pl.multiple_of(WIDE * h, WIDE)
-        out = nt(lhs[0, k], tok_ref[pl.ds(first, 512), :]) + nt(lhs[1, k], tok_ref[pl.ds(first + 512, 512), :])
-        return out.reshape((NZ,) + UNIT)
+        out = nt(lhs[0, k], tok_ref[pl.ds(first, MAIN), :]) + nt(lhs[1, k], tok_ref[pl.ds(first + 512, MAIN), :])
+        return out.reshape(NZ, 24, MAIN)
+
+    def half_b(ref, h):
+        first = pl.multiple_of(WIDE * h, WIDE)
+        for k in range(NX):
+            out = nt(lhs[0, k], tok_ref[pl.ds(first + MAIN, 128), :])
+            out += nt(lhs[1, k], tok_ref[pl.ds(first + 512 + MAIN, 128), :])
+            ref[:, k] = out.reshape(NZ, 24, 128)
 
     loads[2].wait()
     slabs = [(x + 2) % NX, (x + 1) % NX, (x + 3) % NX, x]
@@ -130,23 +138,71 @@
             acc[slabs[1 + side], k] += d2_in[side, i]
         send(acc.at[slabs[1 + side], k], d1_in.at[side, d], d1_s.at[side, d], d1_r.at[side, d], peer_of[side])
 
-    def deliver(d):
+    detour = tuple(jnp.where(c == 0, a, b) for a, b in zip(z_peers[1], z_peers[5]))
+    detoured = jnp.where(c == 0, zat(2), zat(6))
+    relays = {3: (z_peers[0], 0), 5: (z_peers[6], 1), 4: (detour, 2)}
+    directs = {1: 0, 7: 1, 2: 2, 6: 3}
+
+    def relay(block, d, buf, ss, rr):
+        peer, slot = relays[d]
+        send(block, buf.at[slot], ss.at[slot], rr.at[slot], peer)
+
+    def direct(block, d, buf, ss, rr):
+        slot = directs[d]
+        send(block, buf.at[slot], ss.at[slot], rr.at[slot], z_peers[d - 1])
+
+    def settle_x(d):
         for side in range(2):
             arrived(d1_in.at[side, d], d1_r.at[side, d])
         acc[x, zat(d)] += d1_in[0, d] + d1_in[1, d]
-        if d:
-            send(acc.at[x, zat(d)], z_in.at[z], zs.at[d], zr.at[z], z_peers[d - 1])
-
+
+    def deliver(d):
+        settle_x(d)
+        if d in relays:
+            relay(acc.at[x, zat(d)], d, zm_in, zms, zmr)
+        elif d:
+            direct(acc.at[x, zat(d)], d, z_in, zs, zr)
+
+    def deliver_mid():
+        settle_x(2)
+        settle_x(6)
+        for slot, to in enumerate((zat(2), zat(6), detoured)):
+            arrived(zm_in.at[slot], zmr.at[slot])
+            acc[x, to] += zm_in[slot]
+        for d in (2, 6):
+            direct(acc.at[x, zat(d)], d, z_in, zs, zr)
+
+    def deliver_mid_b():
+        for slot, to in enumerate((zat(2), zat(6), detoured)):
+            arrived(bm_in.at[slot], bm_r.at[slot])
+            acc_b[to] += bm_in[slot]
+        for d in (2, 6):
+            direct(acc_b.at[zat(d)], d, bz_in, bz_s, bz_r)
+
+    far_first = (4, 3, 5, 1, 7, 2, 6, 0)
     other[slabs[0]] = half(slabs[0], 1 - c)
+    half_b(other_b, 1 - c)
     pl.semaphore_wait(barrier, len(everyone))
     for i in range(4):
         for side in range(2):
             k, j = zat(halfway[side][i]), 4 * side + i
             send(other.at[slabs[0], k], core_in.at[slabs[0], k], first_s.at[j], first_r.at[j], sib)
+    for d in far_first:
+        send(other_b.at[zat(d)], core_b.at[zat(d)], bc_s.at[d], bc_r.at[d], sib)
     own(0)
-    for i in range(3):
+    half_b(acc_b, c)
+    for i in range(2):
         skip(0, i)
         skip(1, i)
+    for d in far_first:
+        arrived(core_b.at[zat(d)], bc_r.at[d])
+        acc_b[zat(d)] += core_b[zat(d)]
+        if d in relays:
+            relay(acc_b.at[zat(d)], d, bm_in, bm_s, bm_r)
+        elif d in (1, 7):
+            direct(acc_b.at[zat(d)], d, bz_in, bz_s, bz_r)
+    skip(0, 2)
+    skip(1, 2)
     offer(1)
     offer(2)
     own(1)
@@ -172,22 +228,28 @@
     own(3)
     settle(3)
     step(0, 5)
-    step(1, 2)
+    step(1, 5)
     arrived(core_t, core_r.at[0])
     acc_t[...] += core_t[...]
     for d in range(1, NX):
         k = (x + d) % NX
         send(acc_t.at[k], xt_in.at[x], xts.at[d], xtr.at[x], x_peers[d - 1])
     skip(0, 3)
+    step(1, 2)
+    step(0, 2)
     skip(1, 3)
-    step(0, 2)
-    step(1, 5)
+    deliver_mid_b()
     deliver(4)
     deliver(3)
     step(0, 6)
+    step(1, 6)
+    deliver(5)
+    step(0, 1)
     step(1, 1)
-    step(0, 1)
-    step(1, 6)
+    step(0, 7)
+    step(1, 7)
+    step(0, 0)
+    step(1, 0)
     xt = acc_t[x]
     for d in range(1, NX):
         k = (x + d) % NX
@@ -196,24 +258,33 @@
     mine_t[...] = xt
     for d in range(1, NZ):
         send(mine_t, zt_in.at[z], zts.at[d], ztr.at[z], z_peers[d - 1])
-    deliver(5)
-    deliver(2)
-    step(0, 7)
-    step(1, 7)
-    step(0, 0)
-    step(1, 0)
-    deliver(6)
+    gathered = acc_b[z]
+    for slot in range(4):
+        arrived(bz_in.at[slot], bz_r.at[slot])
+        gathered += bz_in[slot]
+    acc_b[z] = gathered
+    for d in range(1, NX):
+        k = (x + d) % NX
+        send(acc_b.at[z, k], bx_in.at[x], bx_s.at[d], bx_r.at[x], x_peers[d - 1])
     deliver(1)
     deliver(7)
+    deliver_mid()
     deliver(0)
+    total_b = acc_b[z, x]
+    for d in range(1, NX):
+        k = (x + d) % NX
+        arrived(bx_in.at[k], bx_r.at[k])
+        total_b += bx_in[k]
     total = acc[x, z]
     total_t = mine_t[...]
     for d in (4, 5, 3, 6, 2, 7, 1):
         k = zat(d)
         arrived(zt_in.at[k], ztr.at[k])
         total_t += zt_in[k]
-        arrived(z_in.at[k], zr.at[k])
-        total += z_in[k]
+    for slot in (0, 1, 3, 2):
+        arrived(z_in.at[slot], zr.at[slot])
+        total += z_in[slot]
+    total = jnp.concatenate([total, total_b], axis=1)
 
     lane = lax.broadcasted_iota(jnp.int32, (16, 128), 1)
     row = lax.broadcasted_iota(jnp.int32, (16, 128), 0)
@@ -375,15 +446,17 @@
             pltpu.VMEM((NX, 128, 256), BF16),
             pltpu.VMEM((64, 2048), BF16),
             pltpu.VMEM((2, 128, 2048), BF16),
-            f32(NX, NZ, *UNIT), f32(NX, NZ, *UNIT), f32(NX, NZ, *UNIT),
+            f32(NX, NZ, 24, MAIN), f32(NX, NZ, 24, MAIN), f32(NX, NZ, 24, MAIN),
+            f32(NZ, NX, 24, 128), f32(NZ, NX, 24, 128), f32(NZ, NX, 24, 128), f32(4, NX, 24, 128), f32(3, NX, 24, 128), f32(NX, 24, 128),
             f32(NX, 16, 128), f32(NX, 16, 128), f32(NX, 16, 128),
-            f32(2, 4, *UNIT), f32(2, NZ, *UNIT), f32(NZ, *UNIT),
+            f32(2, 4, 24, MAIN), f32(2, NZ, 24, MAIN), f32(4, 24, MAIN), f32(3, 24, MAIN),
             f32(NX, 16, 128), f32(NZ, 16, 128), f32(16, 128),
             f32(*UNIT), f32(*UNIT), f32(16, 128), f32(16, 128), f32(16, 128), f32(16, 128),
             f32(8, 24, 128), f32(8, 24, 128), f32(2, NX, 24, 128),
             f32(8, 2 * WIDE + 128), f32(8, 2 * WIDE + 128),
-            dma((8,)), dma((8,)), dma((4,)), dma((4,)), dma((2, 4)), dma((2, 4)), dma((2, NZ)), dma((2, NZ)),
-            dma((NZ,)), dma((NZ,)), dma((NX,)), dma((NX,)), dma((NZ,)), dma((NZ,)), dma((3,)), dma((3,)),
+            dma((8,)), dma((8,)), dma((8,)), dma((8,)), dma((4,)), dma((4,)), dma((3,)), dma((3,)), dma((NX,)), dma((NX,)),
+            dma((4,)), dma((4,)), dma((2, 4)), dma((2, 4)), dma((2, NZ)), dma((2, NZ)),
+            dma((4,)), dma((4,)), dma((3,)), dma((3,)), dma((NX,)), dma((NX,)), dma((NZ,)), dma((NZ,)), dma((3,)), dma((3,)),
             dma((8,)), dma((8,)), dma((8,)), dma((8,)), dma((7,)), dma((2, NX)),
         ],
         compiler_params=pltpu.CompilerParams(

time: 56 us -> 53.7 us (0.959)
  Pallas kernels: 54.6 us -> 52.2 us
    pallas_call x1, Pallas kernels: 53.9 us -> 51.6 us  [per_device(): pl.pallas_call(kernel, out_shape=tuple((pltpu.VMEM(r.shape, r.dtype) for...]
where the time goes in v5:
time: 53.7 us; the launch traced here: 53.5 us
  Pallas kernels  52.2 us (97%)
  between operations  1.28 us (2%)
    pallas_call x1, Pallas kernels, per_device(): pl.pallas_call(kernel, out_shape=tuple((pltpu.VMEM(r.shape, r.dtype) for...  51.6 us

profile of v5, /device:TPU:1, one launch (start us, length us, event | category | flops | bytes accessed | tf_op | source)
XLA Modules:
  0.0 53.5 jit_solution(2458369187223987532)
XLA Ops:
  1.3 51.6 %shard_map.85 = (bf16[6,2080]{1,0:T(8,128)(2,1)S(1)}, f32[6]{0:T(128)S(1)}, f32[2080]{0:T(1024)S(1)}) custom-call(bf16[2080,256]{1,0:T(8,128)(2,1)} %bitcast.1, bf16[256,384]{1,0:T(8,128)(2,1)} %go_hbm.1, s32[1]{0:T(128)S(6)} %copy.9.cnt_hbm, bf16[6,2080]{1,0:T(8,128)(2,1)} %w_hbm.1, f32[6]{0:T(128)} %rs_hbm.1, f32[2080]{0:T(1024)} %cs_hbm.1), custom_call_target="tpu_custom_call" | custom-call | tf_op jit(solution)/shard_map/pallas_call | solution.py:437
  52.9 0.6 %shard_map.86 = (bf16[6,2080]{1,0:T(8,128)(2,1)}, f32[6]{0:T(128)}, f32[2080]{0:T(1024)}) custom-call(bf16[6,2080]{1,0:T(8,128)(2,1)S(1)} %get-tuple-element.6.a, f32[6]{0:T(128)S(1)} %get-tuple-element.7.b, f32[2080]{0:T(1024)S(1)} %get-tuple-element.8.c), custom_call_target="tpu_custom_call" | custom-call | tf_op jit(solution)/shard_map/pallas_call | solution.py:466

commit v6 on v5

--- a/solution.py
+++ b/solution.py
@@ -14,6 +14,7 @@
 PART = 16
 MAIN = 384
 UNIT = (24, 512)
+STATS = 17
 MESH = pl.DeviceIdType.MESH
 F32 = jnp.float32
 BF16 = jnp.bfloat16
@@ -87,7 +88,7 @@
     units = picked.reshape(NX * NZ, 16, 256)
     blank = jnp.zeros((NX * NZ, 8, 256), F32)
     lhs[0] = jnp.concatenate([units, blank], axis=1).reshape(768, 256).astype(BF16).reshape(NX, 192, 256)
-    moved = jnp.concatenate([blank, pltpu.roll(units, 4, 1)], axis=1)
+    moved = jnp.concatenate([blank, pltpu.roll(units[:, 8:16], 4, 1), units[:, 0:8]], axis=1)
     lhs[1] = moved.reshape(768, 256).astype(BF16).reshape(NX, 192, 256)
 
     def half(k, h):
@@ -181,19 +182,19 @@
 
     far_first = (4, 3, 5, 1, 7, 2, 6, 0)
     other[slabs[0]] = half(slabs[0], 1 - c)
-    half_b(other_b, 1 - c)
     pl.semaphore_wait(barrier, len(everyone))
     for i in range(4):
         for side in range(2):
             k, j = zat(halfway[side][i]), 4 * side + i
             send(other.at[slabs[0], k], core_in.at[slabs[0], k], first_s.at[j], first_r.at[j], sib)
+    own(0)
+    half_b(other_b, 1 - c)
     for d in far_first:
         send(other_b.at[zat(d)], core_b.at[zat(d)], bc_s.at[d], bc_r.at[d], sib)
-    own(0)
-    half_b(acc_b, c)
     for i in range(2):
         skip(0, i)
         skip(1, i)
+    half_b(acc_b, c)
     for d in far_first:
         arrived(core_b.at[zat(d)], bc_r.at[d])
         acc_b[zat(d)] += core_b[zat(d)]
@@ -288,7 +289,8 @@
 
     lane = lax.broadcasted_iota(jnp.int32, (16, 128), 1)
     row = lax.broadcasted_iota(jnp.int32, (16, 128), 0)
-    tail = jnp.where((row < ROWS) & (lane // PART == z), total_t, 0.0)
+    tail = jnp.where((row < ROWS) & (lane < PART), pltpu.roll(total_t, (8 - z) % 8 * PART, 1), 0.0)
+    tail_up = jnp.where((row < ROWS) & (lane >= PART) & (lane < 2 * PART), pltpu.roll(total_t, (9 - z) % 8 * PART, 1), 0.0)
     g_own[...] = total
     gt_own[...] = tail
 
@@ -296,12 +298,15 @@
         cp.wait()
     squared = total * total
     squared_t = tail * tail
+    squared_up = tail_up * tail_up
     state = jnp.zeros((16, 128), F32)
     for k in range(OWN):
-        state = jnp.where(row == c * OWN + k, rs_ref[k], state)
+        state = jnp.where(jnp.where(row < ROWS, row, row - 4) == c * OWN + k, rs_ref[k], state)
     sums = jnp.sum(squared, axis=1, keepdims=True)
-    sums = sums[0:16] + jnp.concatenate([sums[12:24], sums[0:4]], axis=0) + jnp.sum(squared_t, axis=1, keepdims=True)
-    r_own[...] = jnp.where(lane < 64, sums, state)
+    sums_t = jnp.sum(squared_t, axis=1, keepdims=True)
+    upper = jnp.broadcast_to(sums[8:16] + sums_t[8:16], (8, 128))
+    r_own[0:8, :] = jnp.where(lane[0:8] < 64, sums[0:8] + sums[16:24] + sums_t[0:8], state[0:8])
+    r_own[8:16, :] = jnp.where(lane[0:8] < 64, upper + pltpu.roll(upper, 4, 0), state[8:16])
     r_copy = send(r_own, r_sib, gs.at[0], gr.at[0], sib)
     g_copy = send(g_own, g_sib, gs.at[1], gr.at[1], sib)
     gt_copy = send(gt_own, gt_sib, gs.at[2], gr.at[2], sib)
@@ -312,24 +317,24 @@
         for h in range(2):
             part = jnp.sum(jnp.where((row24 < ROWS) == (h == 0), values, 0.0), axis=0, keepdims=True)
             for j in range(4):
-                st_a[ma, k + 4 * h + j : k + 4 * h + j + 1, :] = part[:, 128 * j : 128 * (j + 1)]
+                st_a[ma, k + 4 * h + j] = part[:, 128 * j : 128 * (j + 1)]
 
     ma = jnp.where(c == 0, e, z)
     mb = jnp.where(c == 0, z, e)
     columns(squared, 0)
-    st_a[ma, 8:9, :] = jnp.sum(squared_t, axis=0, keepdims=True)
+    tail_c = jnp.sum(squared_t, axis=0, keepdims=True)
     r_copy.wait_recv()
     both = r_own[...] + r_sib[...]
     new_rows = 0.5 * both[:, 64:65] + 0.5 * (both[:, 0:1] / D + 1e-06)
     inverse = 1.0 / new_rows
-    columns(squared * jnp.concatenate([inverse[0:12], inverse[0:12]], axis=0), 9)
-    st_a[ma, 17:18, :] = jnp.sum(squared_t * inverse, axis=0, keepdims=True)
+    columns(squared * jnp.concatenate([inverse, inverse[0:8]], axis=0), 8)
     row_part = jnp.sum(jnp.where(row[:, 0:1] < ROWS, new_rows, 0.0), axis=0, keepdims=True)
-    st_a[ma, 18:24, :] = jnp.broadcast_to(row_part, (6, 128))
+    tail_s = jnp.sum(squared_up * inverse, axis=0, keepdims=True)
+    st_a[ma, 16] = jnp.where(lane[0:1] < 2 * PART, tail_c + tail_s, row_part)
 
     def exchange(buf, me, s, r, peers):
         done = list(started)
-        for d in range(1, 8):
+        for d in (4, 3, 5, 2, 6, 1, 7):
             send(buf.at[me], buf.at[me], s.at[d], r.at[me], peers[d - 1])
         for cp in done:
             cp.wait_send()
@@ -349,21 +354,16 @@
     st_f[c, x] = exchange(st_b, mb, sbs, sbr, [either(b, a) for a, b in zip(y_peers, z_peers)])
     done = list(started)
     started.clear()
-    send(st_f.at[c, x], st_f.at[c, x], sfs.at[6], sfr.at[c, x], sib)
-    for d in range(1, NX):
+    for d in (2, 1, 3):
         send(st_f.at[c, x], st_f.at[c, x], sfs.at[d - 1], sfr.at[c, x], x_peers[d - 1])
         send(st_f.at[c, x], st_f.at[c, x], sfs.at[d + 2], sfr.at[c, x], o_peers[d - 1])
+    send(st_f.at[c, x], st_f.at[c, x], sfs.at[6], sfr.at[c, x], sib)
 
     for cp in done:
         cp.wait_send()
 
     def halves(own, sibling):
         return jnp.where(c == 0, own, sibling), jnp.where(c == 0, sibling, own)
-
-    def fold(v):
-        for shift in (64, 32, 16):
-            v = v + pltpu.roll(v, shift, 1)
-        return v
 
     def rows_of(v, first):
         return jnp.where(c == 0, v[first : first + 6], v[first + 6 : first + 12])
@@ -372,11 +372,13 @@
     gt_copy.wait_recv()
     low, high = halves(g_own[...], g_sib[...])
     for h in range(2):
-        gwide[0:OWN, 512 * h : 512 * (h + 1)] = rows_of(low, ROWS * h)
-        gwide[0:OWN, WIDE + 512 * h : WIDE + 512 * (h + 1)] = rows_of(high, ROWS * h)
-    low, high = halves(fold(gt_own[...]), fold(gt_sib[...]))
-    gwide[0:OWN, 2 * WIDE :] = rows_of(jnp.where(lane < PART, low, high), 0)
+        for first, v in ((512 * h, low), (WIDE + 512 * h, high)):
+            v = jnp.concatenate([v[16:24], v[12:16]], axis=0) if h else v
+            gwide[0:OWN, first : first + 512] = rows_of(v, 0)
+    low, high = halves(gt_own[...], gt_sib[...])
+    gwide[0:OWN, 2 * WIDE :] = rows_of(low + pltpu.roll(high, PART, 1), 0)
     rows6 = rows_of(new_rows, 0)
+    gwide[0:OWN, :] *= lax.rsqrt(rows6)
     eye = lax.broadcasted_iota(jnp.int32, (OWN, 128), 0) == lax.broadcasted_iota(jnp.int32, (OWN, 128), 1)
     nr_ref[...] = jnp.sum(jnp.where(eye, rows6, 0.0), axis=0)[0:OWN]
 
@@ -396,17 +398,17 @@
         for j in range(2):
             for k in range(8):
                 first = WIDE * cc + 128 * k
-                wide[j : j + 1, first : first + 128] = sums[cc][9 * j + k : 9 * j + k + 1]
-    for j in range(2):
-        low, high = (fold(v[9 * j + 8 : 9 * j + 9]) for v in sums)
-        wide[j : j + 1, 2 * WIDE :] = jnp.where(lane[0:1] < PART, low, high)
-    row_avg = sums[0][18:19, 0:1] / FFW
+                wide[j : j + 1, first : first + 128] = sums[cc][8 * j + k]
+    low, high = sums[0][16], sums[1][16]
+    wide[0:1, 2 * WIDE :] = jnp.where(lane[0:1] < PART, low, pltpu.roll(high, PART, 1))
+    wide[1:2, 2 * WIDE :] = jnp.where(lane[0:1] < PART, pltpu.roll(low, 128 - PART, 1), high)
+    row_avg = sums[0][16][:, 2 * PART : 2 * PART + 1] / FFW
     new_cols = 0.5 * cs_ref[...].reshape(1, D) + 0.5 * (wide[0:1, 0:D] / FFW + 1e-06)
     nc_ref[...] = new_cols.reshape(D)
     total_sq = row_avg * jnp.sum(wide[1:2, 0:D] / new_cols, axis=1, keepdims=True)
     rms = jnp.sqrt(total_sq / (FFW * D))
     factor = 0.1 / jnp.maximum(1.0, rms) * jnp.sqrt(row_avg)
-    scaled = gwide[0:OWN, 0:D] * (lax.rsqrt(rows6) * factor) * lax.rsqrt(new_cols)
+    scaled = gwide[0:OWN, 0:D] * (lax.rsqrt(new_cols) * factor)
     nw_ref[...] = (w_ref[...].astype(F32) - scaled).astype(BF16)
 
     for cp in started:
@@ -452,7 +454,7 @@
             f32(2, 4, 24, MAIN), f32(2, NZ, 24, MAIN), f32(4, 24, MAIN), f32(3, 24, MAIN),
             f32(NX, 16, 128), f32(NZ, 16, 128), f32(16, 128),
             f32(*UNIT), f32(*UNIT), f32(16, 128), f32(16, 128), f32(16, 128), f32(16, 128),
-            f32(8, 24, 128), f32(8, 24, 128), f32(2, NX, 24, 128),
+            f32(8, STATS, 1, 128), f32(8, STATS, 1, 128), f32(2, NX, STATS, 1, 128),
             f32(8, 2 * WIDE + 128), f32(8, 2 * WIDE + 128),
             dma((8,)), dma((8,)), dma((8,)), dma((8,)), dma((4,)), dma((4,)), dma((3,)), dma((3,)), dma((NX,)), dma((NX,)),
             dma((4,)), dma((4,)), dma((2, 4)), dma((2, 4)), dma((2, NZ)), dma((2, NZ)),

time: 53.7 us -> 52.4 us (0.976)
  Pallas kernels: 52.2 us -> 50.9 us
    pallas_call x1, Pallas kernels: 51.6 us -> 50.3 us  [per_device(): pl.pallas_call(kernel, out_shape=tuple((pltpu.VMEM(r.shape, r.dtype) for...]
where the time goes in v6:
time: 52.4 us; the launch traced here: 52.2 us
  Pallas kernels  50.9 us (97%)
  between operations  1.28 us (2%)
    pallas_call x1, Pallas kernels, per_device(): pl.pallas_call(kernel, out_shape=tuple((pltpu.VMEM(r.shape, r.dtype) for...  50.3 us

profile of v6, /device:TPU:1, one launch (start us, length us, event | category | flops | bytes accessed | tf_op | source)
XLA Modules:
  0.0 52.2 jit_solution(9022192140072752704)
XLA Ops:
  1.3 50.3 %shard_map.85 = (bf16[6,2080]{1,0:T(8,128)(2,1)S(1)}, f32[6]{0:T(128)S(1)}, f32[2080]{0:T(1024)S(1)}) custom-call(bf16[2080,256]{1,0:T(8,128)(2,1)} %bitcast.1, bf16[256,384]{1,0:T(8,128)(2,1)} %go_hbm.1, s32[1]{0:T(128)S(6)} %copy.9.cnt_hbm, bf16[6,2080]{1,0:T(8,128)(2,1)} %w_hbm.1, f32[6]{0:T(128)} %rs_hbm.1, f32[2080]{0:T(1024)} %cs_hbm.1), custom_call_target="tpu_custom_call" | custom-call | tf_op jit(solution)/shard_map/pallas_call | solution.py:439
  51.6 0.6 %shard_map.86 = (bf16[6,2080]{1,0:T(8,128)(2,1)}, f32[6]{0:T(128)}, f32[2080]{0:T(1024)}) custom-call(bf16[6,2080]{1,0:T(8,128)(2,1)S(1)} %get-tuple-element.6.a, f32[6]{0:T(128)S(1)} %get-tuple-element.7.b, f32[2080]{0:T(1024)S(1)} %get-tuple-element.8.c), custom_call_target="tpu_custom_call" | custom-call | tf_op jit(solution)/shard_map/pallas_call | solution.py:468

commit v7 on v6

--- a/solution.py
+++ b/solution.py
@@ -25,8 +25,8 @@
     nw_ref, nr_ref, nc_ref,
     tok_ref, go_ref, cnt_ref, w_ref, rs_ref, cs_ref, in_s, lhs, picked_t, lhs_t, rhs_t, other, acc, core_in, other_b, acc_b, core_b, bz_in, bm_in, bx_in, other_t, acc_t, core_t, d2_in, d1_in, z_in, zm_in, xt_in, zt_in,
     mine_t, g_own, g_sib, gt_own, gt_sib, r_own, r_sib, st_a, st_b, st_f, wide, gwide,
-    first_s, first_r, bc_s, bc_r, bz_s, bz_r, bm_s, bm_r, bx_s, bx_r, core_s, core_r, d2_s, d2_r, d1_s, d1_r, zs, zr, zms, zmr, xts, xtr, zts, ztr, gs, gr,
-    sas, sar, sbs, sbr, sfs, sfr,
+    core_s, first_r, core_r, bc_s, bc_r, bz_s, bz_r, bm_s, bm_r, bx_s, bx_r, d2_s, d2_r, d1_s, d1_r,
+    zs, zr, zms, zmr, xts, xtr, zts, ztr, gs, gr, sas, sar, sbs, sbr, sfs, sfr,
 ):
     e = lax.axis_index("expert")
     q = lax.axis_index("dp")
@@ -63,10 +63,10 @@
     started = []
 
     def send(*args):
-        cp = remote(*args)
-        cp.start()
-        started.append(cp)
-        return cp
+        remote(*args).start()
+
+    def sent(buf, sem):
+        started.append(remote(buf, buf, sem, sem, sib))
 
     def arrived(buf, sem):
         remote(buf, buf, sem, sem, sib).wait_recv()
@@ -112,7 +112,7 @@
     def offer(j):
         k = slabs[j]
         other[k] = half(k, 1 - c)
-        send(other.at[k], core_in.at[k], core_s.at[j], core_r.at[j], sib)
+        send(other.at[k], core_in.at[k], core_s.at[0], core_r.at[j], sib)
 
     def settle(j):
         k = slabs[j]
@@ -127,9 +127,10 @@
 
     def skip(side, i):
         k = zat(halfway[side][i])
-        arrived(core_in.at[slabs[0], k], first_r.at[4 * side + i])
+        if side == 0 and i % 2 == 0:
+            arrived(core_in.at[0, 0:4], first_r.at[i // 2])
         acc[slabs[0], k] += core_in[slabs[0], k]
-        send(acc.at[slabs[0], k], d2_in.at[side, i], d2_s.at[side, i], d2_r.at[side, i], peer_of[side])
+        send(acc.at[slabs[0], k], d2_in.at[side, i], d2_s, d2_r.at[side, i], peer_of[side])
 
     def step(side, d):
         k = zat(d)
@@ -137,7 +138,7 @@
             i = halfway[side].index(d)
             arrived(d2_in.at[side, i], d2_r.at[side, i])
             acc[slabs[1 + side], k] += d2_in[side, i]
-        send(acc.at[slabs[1 + side], k], d1_in.at[side, d], d1_s.at[side, d], d1_r.at[side, d], peer_of[side])
+        send(acc.at[slabs[1 + side], k], d1_in.at[side, d], d1_s, d1_r.at[d], peer_of[side])
 
     detour = tuple(jnp.where(c == 0, a, b) for a, b in zip(z_peers[1], z_peers[5]))
     detoured = jnp.where(c == 0, zat(2), zat(6))
@@ -146,15 +147,14 @@
 
     def relay(block, d, buf, ss, rr):
         peer, slot = relays[d]
-        send(block, buf.at[slot], ss.at[slot], rr.at[slot], peer)
+        send(block, buf.at[slot], ss, rr, peer)
 
     def direct(block, d, buf, ss, rr):
         slot = directs[d]
-        send(block, buf.at[slot], ss.at[slot], rr.at[slot], z_peers[d - 1])
+        send(block, buf.at[slot], ss, rr, z_peers[d - 1])
 
     def settle_x(d):
-        for side in range(2):
-            arrived(d1_in.at[side, d], d1_r.at[side, d])
+        arrived(d1_in.at[:, d], d1_r.at[d])
         acc[x, zat(d)] += d1_in[0, d] + d1_in[1, d]
 
     def deliver(d):
@@ -167,15 +167,15 @@
     def deliver_mid():
         settle_x(2)
         settle_x(6)
+        arrived(zm_in, zmr)
         for slot, to in enumerate((zat(2), zat(6), detoured)):
-            arrived(zm_in.at[slot], zmr.at[slot])
             acc[x, to] += zm_in[slot]
         for d in (2, 6):
             direct(acc.at[x, zat(d)], d, z_in, zs, zr)
 
     def deliver_mid_b():
+        arrived(bm_in, bm_r)
         for slot, to in enumerate((zat(2), zat(6), detoured)):
-            arrived(bm_in.at[slot], bm_r.at[slot])
             acc_b[to] += bm_in[slot]
         for d in (2, 6):
             direct(acc_b.at[zat(d)], d, bz_in, bz_s, bz_r)
@@ -185,18 +185,21 @@
     pl.semaphore_wait(barrier, len(everyone))
     for i in range(4):
         for side in range(2):
-            k, j = zat(halfway[side][i]), 4 * side + i
-            send(other.at[slabs[0], k], core_in.at[slabs[0], k], first_s.at[j], first_r.at[j], sib)
+            k = zat(halfway[side][i])
+            send(other.at[slabs[0], k], core_in.at[slabs[0], k], core_s.at[0], first_r.at[i // 2], sib)
     own(0)
     half_b(other_b, 1 - c)
     for d in far_first:
-        send(other_b.at[zat(d)], core_b.at[zat(d)], bc_s.at[d], bc_r.at[d], sib)
+        send(other_b.at[zat(d)], core_b.at[zat(d)], bc_s, bc_r.at[0 if d in relays else 1], sib)
     for i in range(2):
         skip(0, i)
         skip(1, i)
     half_b(acc_b, c)
     for d in far_first:
-        arrived(core_b.at[zat(d)], bc_r.at[d])
+        if d == far_first[0]:
+            arrived(core_b.at[0:3], bc_r.at[0])
+        if d == far_first[3]:
+            arrived(core_b.at[0:5], bc_r.at[1])
         acc_b[zat(d)] += core_b[zat(d)]
         if d in relays:
             relay(acc_b.at[zat(d)], d, bm_in, bm_s, bm_r)
@@ -224,7 +227,7 @@
                 2 * WIDE + PART * h : 2 * WIDE + PART * (h + 1), :
             ]
     other_t[...] = nt(lhs_t[...], rhs_t[1 - c]).reshape(NX, 16, 128)
-    send(other_t, core_t, core_s.at[0], core_r.at[0], sib)
+    send(other_t, core_t, core_s.at[1], core_r.at[0], sib)
     acc_t[...] = nt(lhs_t[...], rhs_t[c]).reshape(NX, 16, 128)
     own(3)
     settle(3)
@@ -234,7 +237,7 @@
     acc_t[...] += core_t[...]
     for d in range(1, NX):
         k = (x + d) % NX
-        send(acc_t.at[k], xt_in.at[x], xts.at[d], xtr.at[x], x_peers[d - 1])
+        send(acc_t.at[k], xt_in.at[x], xts, xtr, x_peers[d - 1])
     skip(0, 3)
     step(1, 2)
     step(0, 2)
@@ -252,38 +255,40 @@
     step(0, 0)
     step(1, 0)
     xt = acc_t[x]
+    arrived(xt_in.at[0:3], xtr)
     for d in range(1, NX):
-        k = (x + d) % NX
-        arrived(xt_in.at[k], xtr.at[k])
-        xt += xt_in[k]
+        xt += xt_in[(x + d) % NX]
     mine_t[...] = xt
     for d in range(1, NZ):
-        send(mine_t, zt_in.at[z], zts.at[d], ztr.at[z], z_peers[d - 1])
+        send(mine_t, zt_in.at[z], zts, ztr, z_peers[d - 1])
     gathered = acc_b[z]
+    arrived(bz_in, bz_r)
     for slot in range(4):
-        arrived(bz_in.at[slot], bz_r.at[slot])
         gathered += bz_in[slot]
     acc_b[z] = gathered
     for d in range(1, NX):
         k = (x + d) % NX
-        send(acc_b.at[z, k], bx_in.at[x], bx_s.at[d], bx_r.at[x], x_peers[d - 1])
+        send(acc_b.at[z, k], bx_in.at[x], bx_s, bx_r, x_peers[d - 1])
     deliver(1)
     deliver(7)
     deliver_mid()
     deliver(0)
+    for buf, sem in (
+        (other, core_s.at[0]), (other_t, core_s.at[1]), (other_b, bc_s), (d2_in, d2_s), (d1_in, d1_s), (xt_in.at[0:3], xts),
+        (zt_in.at[0:7], zts), (bm_in, bm_s), (bz_in, bz_s), (bx_in.at[0:3], bx_s), (zm_in, zms), (z_in, zs),
+    ):
+        sent(buf, sem)
     total_b = acc_b[z, x]
+    arrived(bx_in.at[0:3], bx_r)
     for d in range(1, NX):
-        k = (x + d) % NX
-        arrived(bx_in.at[k], bx_r.at[k])
-        total_b += bx_in[k]
+        total_b += bx_in[(x + d) % NX]
     total = acc[x, z]
     total_t = mine_t[...]
+    arrived(zt_in.at[0:7], ztr)
     for d in (4, 5, 3, 6, 2, 7, 1):
-        k = zat(d)
-        arrived(zt_in.at[k], ztr.at[k])
-        total_t += zt_in[k]
-    for slot in (0, 1, 3, 2):
-        arrived(z_in.at[slot], zr.at[slot])
+        total_t += zt_in[zat(d)]
+    arrived(z_in, zr)
+    for slot in range(4):
         total += z_in[slot]
     total = jnp.concatenate([total, total_b], axis=1)
 
@@ -307,9 +312,13 @@
     upper = jnp.broadcast_to(sums[8:16] + sums_t[8:16], (8, 128))
     r_own[0:8, :] = jnp.where(lane[0:8] < 64, sums[0:8] + sums[16:24] + sums_t[0:8], state[0:8])
     r_own[8:16, :] = jnp.where(lane[0:8] < 64, upper + pltpu.roll(upper, 4, 0), state[8:16])
-    r_copy = send(r_own, r_sib, gs.at[0], gr.at[0], sib)
-    g_copy = send(g_own, g_sib, gs.at[1], gr.at[1], sib)
-    gt_copy = send(gt_own, gt_sib, gs.at[2], gr.at[2], sib)
+    r_copy, g_copy, gt_copy = (
+        remote(src, dst, gs.at[k], gr.at[k], sib)
+        for k, (src, dst) in enumerate([(r_own, r_sib), (g_own, g_sib), (gt_own, gt_sib)])
+    )
+    for cp in (r_copy, g_copy, gt_copy):
+        cp.start()
+        started.append(cp)
 
     row24 = lax.broadcasted_iota(jnp.int32, (24, 1), 0)
 
@@ -333,15 +342,13 @@
     st_a[ma, 16] = jnp.where(lane[0:1] < 2 * PART, tail_c + tail_s, row_part)
 
     def exchange(buf, me, s, r, peers):
-        done = list(started)
         for d in (4, 3, 5, 2, 6, 1, 7):
-            send(buf.at[me], buf.at[me], s.at[d], r.at[me], peers[d - 1])
-        for cp in done:
+            send(buf.at[me], buf.at[me], s, r, peers[d - 1])
+        for cp in started:
             cp.wait_send()
-            started.remove(cp)
-        for d in (7, 1, 6, 2, 5, 3, 4):
-            k = (me + d) % 8
-            arrived(buf.at[k], r.at[k])
+        started.clear()
+        sent(buf.at[0:7], s)
+        arrived(buf.at[0:7], r)
         out = buf[0]
         for k in range(1, 8):
             out += buf[k]
@@ -352,15 +359,14 @@
 
     st_b[mb] = exchange(st_a, ma, sas, sar, [either(a, b) for a, b in zip(y_peers, z_peers)])
     st_f[c, x] = exchange(st_b, mb, sbs, sbr, [either(b, a) for a, b in zip(y_peers, z_peers)])
-    done = list(started)
+    for d in (2, 1, 3):
+        send(st_f.at[c, x], st_f.at[c, x], sfs, sfr, x_peers[d - 1])
+        send(st_f.at[c, x], st_f.at[c, x], sfs, sfr, o_peers[d - 1])
+    send(st_f.at[c, x], st_f.at[c, x], sfs, sfr, sib)
+    for cp in started:
+        cp.wait_send()
     started.clear()
-    for d in (2, 1, 3):
-        send(st_f.at[c, x], st_f.at[c, x], sfs.at[d - 1], sfr.at[c, x], x_peers[d - 1])
-        send(st_f.at[c, x], st_f.at[c, x], sfs.at[d + 2], sfr.at[c, x], o_peers[d - 1])
-    send(st_f.at[c, x], st_f.at[c, x], sfs.at[6], sfr.at[c, x], sib)
-
-    for cp in done:
-        cp.wait_send()
+    sent(st_a.at[0:7], sfs)
 
     def halves(own, sibling):
         return jnp.where(c == 0, own, sibling), jnp.where(c == 0, sibling, own)
@@ -382,12 +388,7 @@
     eye = lax.broadcasted_iota(jnp.int32, (OWN, 128), 0) == lax.broadcasted_iota(jnp.int32, (OWN, 128), 1)
     nr_ref[...] = jnp.sum(jnp.where(eye, rows6, 0.0), axis=0)[0:OWN]
 
-    arrived(st_f.at[1 - c, x], sfr.at[1 - c, x])
-    for d in range(1, NX):
-        for cc in range(2):
-            k = (x + d) % NX
-            core_k = (c + cc) % 2
-            arrived(st_f.at[core_k, k], sfr.at[core_k, k])
+    arrived(st_a.at[0:7], sfr)
     sums = []
     for cc in range(2):
         v = st_f[cc, 0]
@@ -456,10 +457,10 @@
             f32(*UNIT), f32(*UNIT), f32(16, 128), f32(16, 128), f32(16, 128), f32(16, 128),
             f32(8, STATS, 1, 128), f32(8, STATS, 1, 128), f32(2, NX, STATS, 1, 128),
             f32(8, 2 * WIDE + 128), f32(8, 2 * WIDE + 128),
-            dma((8,)), dma((8,)), dma((8,)), dma((8,)), dma((4,)), dma((4,)), dma((3,)), dma((3,)), dma((NX,)), dma((NX,)),
-            dma((4,)), dma((4,)), dma((2, 4)), dma((2, 4)), dma((2, NZ)), dma((2, NZ)),
-            dma((4,)), dma((4,)), dma((3,)), dma((3,)), dma((NX,)), dma((NX,)), dma((NZ,)), dma((NZ,)), dma((3,)), dma((3,)),
-            dma((8,)), dma((8,)), dma((8,)), dma((8,)), dma((7,)), dma((2, NX)),
+            dma((2,)), dma((2,)), dma((4,)), dma(()), dma((2,)), dma(()), dma(()), dma(()), dma(()), dma(()), dma(()),
+            dma(()), dma((2, 4)), dma(()), dma((8,)),
+            dma(()), dma(()), dma(()), dma(()), dma(()), dma(()), dma(()), dma(()), dma((3,)), dma((3,)),
+            dma(()), dma(()), dma(()), dma(()), dma(()), dma(()),
         ],
         compiler_params=pltpu.CompilerParams(
             collective_id=0, has_side_effects=True, vmem_limit_bytes=56 * 2**20

time: 52.4 us -> 51 us (0.973)
  Pallas kernels: 50.9 us -> 49.6 us
    pallas_call x1, Pallas kernels: 50.3 us -> 49 us  [per_device(): pl.pallas_call(kernel, out_shape=tuple((pltpu.VMEM(r.shape, r.dtype) for...]
where the time goes in v7:
time: 51 us; the launch traced here: 50.9 us
  Pallas kernels  49.6 us (97%)
  between operations  1.28 us (3%)
    pallas_call x1, Pallas kernels, per_device(): pl.pallas_call(kernel, out_shape=tuple((pltpu.VMEM(r.shape, r.dtype) for...  49 us

profile of v7, /device:TPU:1, one launch (start us, length us, event | category | flops | bytes accessed | tf_op | source)
XLA Modules:
  0.0 50.9 jit_solution(15988569364804395674)
XLA Ops:
  1.3 49.0 %shard_map.85 = (bf16[6,2080]{1,0:T(8,128)(2,1)S(1)}, f32[6]{0:T(128)S(1)}, f32[2080]{0:T(1024)S(1)}) custom-call(bf16[2080,256]{1,0:T(8,128)(2,1)} %bitcast.1, bf16[256,384]{1,0:T(8,128)(2,1)} %go_hbm.1, s32[1]{0:T(128)S(6)} %copy.9.cnt_hbm, bf16[6,2080]{1,0:T(8,128)(2,1)} %w_hbm.1, f32[6]{0:T(128)} %rs_hbm.1, f32[2080]{0:T(1024)} %cs_hbm.1), custom_call_target="tpu_custom_call" | custom-call | tf_op jit(solution)/shard_map/pallas_call | solution.py:440
  50.2 0.6 %shard_map.86 = (bf16[6,2080]{1,0:T(8,128)(2,1)}, f32[6]{0:T(128)}, f32[2080]{0:T(1024)}) custom-call(bf16[6,2080]{1,0:T(8,128)(2,1)S(1)} %get-tuple-element.6.a, f32[6]{0:T(128)S(1)} %get-tuple-element.7.b, f32[2080]{0:T(1024)S(1)} %get-tuple-element.8.c), custom_call_target="tpu_custom_call" | custom-call | tf_op jit(solution)/shard_map/pallas_call | solution.py:469

commit v8 on v7

--- a/solution.py
+++ b/solution.py
@@ -23,7 +23,7 @@
 def kernel(
     tok_hbm, go_hbm, cnt_hbm, w_hbm, rs_hbm, cs_hbm,
     nw_ref, nr_ref, nc_ref,
-    tok_ref, go_ref, cnt_ref, w_ref, rs_ref, cs_ref, in_s, lhs, picked_t, lhs_t, rhs_t, other, acc, core_in, other_b, acc_b, core_b, bz_in, bm_in, bx_in, other_t, acc_t, core_t, d2_in, d1_in, z_in, zm_in, xt_in, zt_in,
+    tok_ref, go_ref, cnt_ref, w_ref, rs_ref, cs_ref, in_s, lhs, picked, lhs_t, rhs_t, other, acc, core_in, other_b, acc_b, core_b, bz_in, bm_in, bx_in, other_t, acc_t, core_t, d2_in, d1_in, z_in, zm_in, xt_in, zt_in,
     mine_t, g_own, g_sib, gt_own, gt_sib, r_own, r_sib, st_a, st_b, st_f, wide, gwide,
     core_s, first_r, core_r, bc_s, bc_r, bz_s, bz_r, bm_s, bm_r, bx_s, bx_r, d2_s, d2_r, d1_s, d1_r,
     zs, zr, zms, zmr, xts, xtr, zts, ztr, gs, gr, sas, sar, sbs, sbr, sfs, sfr,
@@ -83,13 +83,17 @@
     loads[1].wait()
     live = lax.broadcasted_iota(jnp.int32, (256, 384), 0) < cnt_ref[0]
     masked = jnp.where(live, go_ref[...].astype(F32), 0.0).astype(BF16)
-    picked = nt(pick, masked)
-    picked_t[...] = picked.astype(BF16).reshape(NX, 128, 256)
-    units = picked.reshape(NX * NZ, 16, 256)
-    blank = jnp.zeros((NX * NZ, 8, 256), F32)
-    lhs[0] = jnp.concatenate([units, blank], axis=1).reshape(768, 256).astype(BF16).reshape(NX, 192, 256)
-    moved = jnp.concatenate([blank, pltpu.roll(units[:, 8:16], 4, 1), units[:, 0:8]], axis=1)
-    lhs[1] = moved.reshape(768, 256).astype(BF16).reshape(NX, 192, 256)
+    picked[...] = nt(pick, masked).reshape(NX, 128, 256)
+
+    def build(k):
+        units = picked[k].reshape(NZ, 16, 256)
+        blank = jnp.zeros((NZ, 8, 256), F32)
+        lhs[0, k] = jnp.concatenate([units, blank], axis=1).reshape(192, 256).astype(BF16)
+        moved = jnp.concatenate([blank, pltpu.roll(units[:, 8:16], 4, 1), units[:, 0:8]], axis=1)
+        lhs[1, k] = moved.reshape(192, 256).astype(BF16)
+
+    slabs = [(x + 2) % NX, (x + 1) % NX, (x + 3) % NX, x]
+    build(slabs[0])
 
     def half(k, h):
         first = pl.multiple_of(WIDE * h, WIDE)
@@ -98,13 +102,12 @@
 
     def half_b(ref, h):
         first = pl.multiple_of(WIDE * h, WIDE)
+        out = nt(lhs[0].reshape(768, 256), tok_ref[pl.ds(first + MAIN, 128), :])
+        out += nt(lhs[1].reshape(768, 256), tok_ref[pl.ds(first + 512 + MAIN, 128), :])
         for k in range(NX):
-            out = nt(lhs[0, k], tok_ref[pl.ds(first + MAIN, 128), :])
-            out += nt(lhs[1, k], tok_ref[pl.ds(first + 512 + MAIN, 128), :])
-            ref[:, k] = out.reshape(NZ, 24, 128)
+            ref[:, k] = out[192 * k : 192 * (k + 1)].reshape(NZ, 24, 128)
 
     loads[2].wait()
-    slabs = [(x + 2) % NX, (x + 1) % NX, (x + 3) % NX, x]
 
     def zat(d):
         return (z + d) % NZ
@@ -188,12 +191,16 @@
             k = zat(halfway[side][i])
             send(other.at[slabs[0], k], core_in.at[slabs[0], k], core_s.at[0], first_r.at[i // 2], sib)
     own(0)
+    for k in slabs[1:]:
+        build(k)
     half_b(other_b, 1 - c)
     for d in far_first:
         send(other_b.at[zat(d)], core_b.at[zat(d)], bc_s, bc_r.at[0 if d in relays else 1], sib)
-    for i in range(2):
+    for i in range(3):
         skip(0, i)
         skip(1, i)
+    offer(1)
+    offer(2)
     half_b(acc_b, c)
     for d in far_first:
         if d == far_first[0]:
@@ -205,23 +212,25 @@
             relay(acc_b.at[zat(d)], d, bm_in, bm_s, bm_r)
         elif d in (1, 7):
             direct(acc_b.at[zat(d)], d, bz_in, bz_s, bz_r)
-    skip(0, 2)
-    skip(1, 2)
-    offer(1)
-    offer(2)
     own(1)
     settle(1)
     step(0, 3)
     own(2)
     settle(2)
     step(1, 4)
+    offer(3)
     step(0, 4)
     step(1, 3)
-    offer(3)
+    step(0, 5)
+    step(1, 5)
+    skip(0, 3)
+    skip(1, 3)
+    step(1, 2)
+    step(0, 2)
     rhs_t[...] = jnp.zeros_like(rhs_t)
     for k in range(NZ):
         for j in range(NX):
-            lhs_t[16 * j : 16 * (j + 1), 256 * k : 256 * (k + 1)] = picked_t[j, 16 * k : 16 * (k + 1), :]
+            lhs_t[16 * j : 16 * (j + 1), 256 * k : 256 * (k + 1)] = picked[j, 16 * k : 16 * (k + 1), :].astype(BF16)
         for h in range(2):
             rhs_t[h, PART * k : PART * (k + 1), 256 * k : 256 * (k + 1)] = tok_ref[
                 2 * WIDE + PART * h : 2 * WIDE + PART * (h + 1), :
@@ -231,25 +240,19 @@
     acc_t[...] = nt(lhs_t[...], rhs_t[c]).reshape(NX, 16, 128)
     own(3)
     settle(3)
-    step(0, 5)
-    step(1, 5)
     arrived(core_t, core_r.at[0])
     acc_t[...] += core_t[...]
     for d in range(1, NX):
         k = (x + d) % NX
         send(acc_t.at[k], xt_in.at[x], xts, xtr, x_peers[d - 1])
-    skip(0, 3)
-    step(1, 2)
-    step(0, 2)
-    skip(1, 3)
+    step(0, 6)
+    step(1, 6)
     deliver_mid_b()
     deliver(4)
     deliver(3)
-    step(0, 6)
-    step(1, 6)
-    deliver(5)
     step(0, 1)
     step(1, 1)
+    deliver(5)
     step(0, 7)
     step(1, 7)
     step(0, 0)
@@ -446,7 +449,7 @@
             pltpu.VMEM((D, 256), BF16), pltpu.VMEM((256, 384), BF16), pltpu.SMEM((1,), jnp.int32),
             pltpu.VMEM((OWN, D), BF16), pltpu.SMEM((OWN,), F32), pltpu.VMEM((D,), F32), dma((6,)),
             pltpu.VMEM((2, NX, 192, 256), BF16),
-            pltpu.VMEM((NX, 128, 256), BF16),
+            f32(NX, 128, 256),
             pltpu.VMEM((64, 2048), BF16),
             pltpu.VMEM((2, 128, 2048), BF16),
             f32(NX, NZ, 24, MAIN), f32(NX, NZ, 24, MAIN), f32(NX, NZ, 24, MAIN),

time: 51 us -> 50.2 us (0.984)
  Pallas kernels: 49.6 us -> 48.7 us
    pallas_call x1, Pallas kernels: 49 us -> 48.1 us  [per_device(): pl.pallas_call(kernel, out_shape=tuple((pltpu.VMEM(r.shape, r.dtype) for...]
where the time goes in v8:
time: 50.2 us; the launch traced here: 50 us
  Pallas kernels  48.7 us (97%)
  between operations  1.28 us (3%)
    pallas_call x1, Pallas kernels, per_device(): pl.pallas_call(kernel, out_shape=tuple((pltpu.VMEM(r.shape, r.dtype) for...  48.1 us

profile of v8, /device:TPU:1, one launch (start us, length us, event | category | flops | bytes accessed | tf_op | source)
XLA Modules:
  0.0 50.0 jit_solution(12293345118259956143)
XLA Ops:
  1.3 48.1 %shard_map.85 = (bf16[6,2080]{1,0:T(8,128)(2,1)S(1)}, f32[6]{0:T(128)S(1)}, f32[2080]{0:T(1024)S(1)}) custom-call(bf16[2080,256]{1,0:T(8,128)(2,1)} %bitcast.1, bf16[256,384]{1,0:T(8,128)(2,1)} %go_hbm.1, s32[1]{0:T(128)S(6)} %copy.9.cnt_hbm, bf16[6,2080]{1,0:T(8,128)(2,1)} %w_hbm.1, f32[6]{0:T(128)} %rs_hbm.1, f32[2080]{0:T(1024)} %cs_hbm.1), custom_call_target="tpu_custom_call" | custom-call | tf_op jit(solution)/shard_map/pallas_call | solution.py:443
  49.4 0.6 %shard_map.86 = (bf16[6,2080]{1,0:T(8,128)(2,1)}, f32[6]{0:T(128)}, f32[2080]{0:T(1024)}) custom-call(bf16[6,2080]{1,0:T(8,128)(2,1)S(1)} %get-tuple-element.6.a, f32[6]{0:T(128)S(1)} %get-tuple-element.7.b, f32[2080]{0:T(1024)S(1)} %get-tuple-element.8.c), custom_call_target="tpu_custom_call" | custom-call | tf_op jit(solution)/shard_map/pallas_call | solution.py:472

commit v9 on v8

--- a/solution.py
+++ b/solution.py
@@ -51,7 +51,7 @@
     for cp in loads:
         cp.start()
     barrier = pltpu.get_barrier_semaphore()
-    everyone = [sib] + y_peers + z_peers + x_peers + o_peers
+    everyone = [p[d - 1] for d in (4, 3, 5, 2, 6, 1, 7) for p in (y_peers, z_peers)] + x_peers + o_peers + [sib]
     for peer in everyone:
         pl.semaphore_signal(barrier, inc=1, device_id=peer, device_id_type=MESH)
 
@@ -264,6 +264,8 @@
     mine_t[...] = xt
     for d in range(1, NZ):
         send(mine_t, zt_in.at[z], zts, ztr, z_peers[d - 1])
+    deliver(1)
+    deliver(7)
     gathered = acc_b[z]
     arrived(bz_in, bz_r)
     for slot in range(4):
@@ -272,8 +274,6 @@
     for d in range(1, NX):
         k = (x + d) % NX
         send(acc_b.at[z, k], bx_in.at[x], bx_s, bx_r, x_peers[d - 1])
-    deliver(1)
-    deliver(7)
     deliver_mid()
     deliver(0)
     for buf, sem in (

time: 50.2 us -> 50.2 us (level)
  no operation moved by 1% of the time
where the time goes in v9:
time: 50.2 us; the launch traced here: 50 us
  Pallas kernels  48.7 us (97%)
  between operations  1.28 us (3%)
    pallas_call x1, Pallas kernels, per_device(): pl.pallas_call(kernel, out_shape=tuple((pltpu.VMEM(r.shape, r.dtype) for...  48.1 us

profile of v9, /device:TPU:1, one launch (start us, length us, event | category | flops | bytes accessed | tf_op | source)
XLA Modules:
  0.0 50.0 jit_solution(6892886532600943791)
XLA Ops:
  1.3 48.1 %shard_map.85 = (bf16[6,2080]{1,0:T(8,128)(2,1)S(1)}, f32[6]{0:T(128)S(1)}, f32[2080]{0:T(1024)S(1)}) custom-call(bf16[2080,256]{1,0:T(8,128)(2,1)} %bitcast.1, bf16[256,384]{1,0:T(8,128)(2,1)} %go_hbm.1, s32[1]{0:T(128)S(6)} %copy.9.cnt_hbm, bf16[6,2080]{1,0:T(8,128)(2,1)} %w_hbm.1, f32[6]{0:T(128)} %rs_hbm.1, f32[2080]{0:T(1024)} %cs_hbm.1), custom_call_target="tpu_custom_call" | custom-call | tf_op jit(solution)/shard_map/pallas_call | solution.py:443
  49.4 0.6 %shard_map.86 = (bf16[6,2080]{1,0:T(8,128)(2,1)}, f32[6]{0:T(128)}, f32[2080]{0:T(1024)}) custom-call(bf16[6,2080]{1,0:T(8,128)(2,1)S(1)} %get-tuple-element.6.a, f32[6]{0:T(128)S(1)} %get-tuple-element.7.b, f32[2080]{0:T(1024)S(1)} %get-tuple-element.8.c), custom_call_target="tpu_custom_call" | custom-call | tf_op jit(solution)/shard_map/pallas_call | solution.py:472
